TPU v7x, 256 devices: a whole 4x4x8 slice. The times are simulated.
256 devices in a mesh: grp: 8 (over z), tile: 32 (over x, y, core).
Axes of the slice: x: 4, y: 4, z: 8, core: 2. Of those that a mesh axis runs over, the one named last changes fastest.
Arguments:
- spot_terms: bfloat16 [65536, 1024], P('tile', 'grp'), may hold values from -6 to 6
- spot_weight: bfloat16 [65536], P('tile'), may hold values from 0.29882812 to 3
- spot_owner: int32 [65536, 1], P('tile'), may hold values from 0 to 31, as said below
- spot_cell: int32 [65536], P('tile'), may hold values from 0 to 1023
- col_coef: float32 [32, 1024], P('tile'), may hold values from 0.04 to 0.45
- row_coef: float32 [32, 1024], P('tile'), may hold values from 0.04 to 0.45
- tgt_coef: float32 [1024], P('grp'), may hold values from 0.03 to 0.24
- tgt_weight: float32 [1024], P('grp'), may hold values from 0.5 to 6
Outputs:
- new_plan: float32 [32, 1024, 1024], P('tile', None, 'grp')
Inputs may be any that keep to these rules, and one draw needn't show every extreme that they name: `spot_owner`: among the 2048 spots of one device no owner is named more than 128 times, and in every device's block some owner is named exactly 128 times.
All inputs are finite; a program needn't handle non-finite values.
Results may differ from a plain program's by a relative error of at most 0.0003.
Values may be sent and summed in bfloat16 or wider, within the bound.
No kernel may reach another device: no remote copies, remote signals or barrier semaphores. Data moves between devices by JAX's collectives and lax.ppermute only.
A program may use at most 64 MiB of HBM per device.

v0:
```python
import jax
import jax.numpy as jnp
from jax import lax
from jax.sharding import PartitionSpec as P

PATCH_ROW = 32
HEAT_STEPS = 10
SCALING_ROUNDS = 5


EXPONENT_GAIN = 2.0


def padded_2(cells, sides, width):
    for axis, dim in sides:
        count = lax.axis_size(axis)
        ends = count - 1
        head = lax.slice_in_dim(cells, 0, width, axis=dim)
        tail = lax.slice_in_dim(cells, cells.shape[dim] - width, cells.shape[dim], axis=dim)
        cells = jnp.concatenate(
            [
                lax.ppermute(tail, axis, [(i, (i + 1) % count) for i in range(ends)]),
                cells,
                lax.ppermute(head, axis, [((i + 1) % count, i) for i in range(ends)]),
            ],
            axis=dim,
        )
    return cells


def shifted(values, offset, along_axis):
    length = values.shape[along_axis]
    filler_shape = list(values.shape)
    filler_shape[along_axis] = abs(offset)
    padding_value = jnp.zeros(filler_shape, values.dtype)
    if offset > 0:
        kept_part = lax.slice_in_dim(values, 0, length - offset, axis=along_axis)
        return jnp.concatenate([padding_value, kept_part], axis=along_axis)
    kept_part = lax.slice_in_dim(values, -offset, length, axis=along_axis)
    return jnp.concatenate([kept_part, padding_value], axis=along_axis)


def line_heat(values, coefficient, along_axis):

    def line_heat_once(step_index, current):
        beside = shifted(current, 1, along_axis) + shifted(current, -1, along_axis)
        return current + coefficient * (beside - 2.0 * current)

    return lax.fori_loop(0, HEAT_STEPS, line_heat_once, values)


def patch_heat(values, coefficient):
    last_axis = values.ndim - 1
    positions = jnp.arange(values.shape[-1], dtype=jnp.int32) % PATCH_ROW
    west_valid = positions > 0
    east_valid = positions < PATCH_ROW - 1

    def patch_heat_once(step_index, current):
        western_edge = jnp.where(west_valid, shifted(current, 1, last_axis), 0.0)
        east_side = jnp.where(east_valid, shifted(current, -1, last_axis), 0.0)
        north_side = shifted(current, PATCH_ROW, last_axis)
        south_side = shifted(current, -PATCH_ROW, last_axis)
        beside = western_edge + east_side + north_side + south_side
        return current + coefficient * (beside - 4.0 * current)

    return lax.fori_loop(0, HEAT_STEPS, patch_heat_once, values)


def scale_plan(gibbs_kernel, cell_mass, tgt_weight, tile_count):
    col_scale = jnp.ones((gibbs_kernel.shape[1],), jnp.float32)
    row_scale = jnp.zeros((gibbs_kernel.shape[0],), jnp.float32)
    for scaling_round in range(SCALING_ROUNDS):
        partial_rows = jnp.dot(gibbs_kernel, col_scale, precision=lax.Precision.HIGHEST)
        row_sums = lax.psum(partial_rows, "grp")
        row_scale = cell_mass / row_sums
        partial_cols = jnp.dot(row_scale, gibbs_kernel, precision=lax.Precision.HIGHEST)
        col_sums = lax.psum(partial_cols, "tile")
        col_scale = tgt_weight / col_sums
    return (
        row_scale[:, None]
        * gibbs_kernel
        * col_scale[None, :]
        * float(gibbs_kernel.shape[0] * tile_count)
    )


def body(spot_terms, spot_weight, spot_owner, spot_cell, col_coef, row_coef, tgt_coef, tgt_weight):
    tile_count = lax.axis_size("tile")
    column_count = spot_terms.shape[1]
    capacity = 2 * spot_terms.shape[0] // tile_count
    rows_here = col_coef.shape[0]
    width_here = col_coef.shape[1]
    owner_index = spot_owner[:, 0]
    member = (owner_index[:, None] == jnp.arange(tile_count, dtype=jnp.int32)[None, :]).astype(
        jnp.int32
    )
    before = jnp.cumsum(member, axis=0) - member
    slot_rank = jnp.sum(before * member, axis=1)
    target_slot = owner_index * capacity + slot_rank
    slot_total = tile_count * capacity
    outgoing = jnp.zeros((slot_total, column_count), jnp.bfloat16).at[target_slot].set(spot_terms)
    outgoing = outgoing.reshape(tile_count, capacity, column_count)
    out_weight = jnp.zeros((slot_total,), jnp.bfloat16).at[target_slot].set(spot_weight)
    out_weight = out_weight.reshape(tile_count, capacity)
    out_cell = jnp.zeros((slot_total,), jnp.int32).at[target_slot].set(spot_cell)
    out_cell = out_cell.reshape(tile_count, capacity)
    got_rows, got_weight = (
        lax.all_to_all(outgoing, "tile", split_axis=0, concat_axis=0, tiled=True),
        lax.all_to_all(out_weight, "tile", split_axis=0, concat_axis=0, tiled=True),
    )
    got_cell = lax.all_to_all(out_cell, "tile", split_axis=0, concat_axis=0, tiled=True)
    flat_cell = got_cell.reshape(-1)
    cells_local = rows_here * width_here
    plan_field = jnp.zeros((cells_local, column_count), jnp.float32)
    plan_field = plan_field.at[flat_cell].add(
        got_rows.reshape(-1, column_count).astype(jnp.float32)
    )
    plan_field = plan_field.reshape(rows_here, width_here, column_count)
    cell_mass = (
        jnp.zeros((cells_local,), jnp.float32)
        .at[flat_cell]
        .add(got_weight.reshape(-1).astype(jnp.float32))
    )
    cell_mass = cell_mass.reshape(rows_here, width_here)
    plan_field = line_heat(plan_field, col_coef[:, :, None], 1)

    def rim_step(step_index, current):
        padded = padded_2(current, (("tile", 0),), 1)
        return current + row_coef[:, :, None] * (padded[2:] + padded[:-2] - 2.0 * current)

    plan_field = lax.fori_loop(0, HEAT_STEPS, rim_step, plan_field)
    plan_field = patch_heat(plan_field, tgt_coef)
    gibbs_kernel = jnp.exp(EXPONENT_GAIN * plan_field)
    new_plan = scale_plan(
        gibbs_kernel.reshape(-1, column_count), cell_mass.reshape(-1), tgt_weight, tile_count
    )
    new_plan = new_plan.reshape(plan_field.shape)
    return new_plan


def solution(mesh):
    return jax.shard_map(
        body,
        mesh=mesh,
        in_specs=(
            P("tile", "grp"),
            P("tile"),
            P("tile", None),
            P("tile"),
            P("tile", None),
            P("tile", None),
            P("grp"),
            P("grp"),
        ),
        out_specs=P("tile", None, "grp"),
        check_vma=False,
    )
```

profile of v0, /device:TPU:1, one launch (start us, length us, event | category | flops | bytes accessed | tf_op | source)
XLA Modules:
  0.0 673.9 jit_solution(10218841312935247736)
XLA Ops:
  0.8 9.1 %reduce-window.6 = s32[32,16,128]{2,1,0:T(8,128)S(1)} reduce-window(s32[32,16,128]{2,1,0:T(8,128)S(1)} %fusion.27, s32[]{:T(128)} %copy.36), window={size=1x1x128 pad=0_0x0_0x127_0}, to_apply=%region_0.0 | reduce-window | flops 8323072 | bytes 524292 | tf_op jit(solution)/shard_map/reduce-window
  10.7 14.8 %scatter_custom_fusion.1 = bf16[4096]{0:T(1024)(128)(2,1)S(1)} fusion(s32[2048]{0:T(1024)S(1)} %bitcast.127, bf16[2048]{0:T(1024)(128)(2,1)} %param.15, bf16[]{:T(256)} %constant.39.clone.1), kind=kCustom, calls=%fused_computation.52 | custom fusion | bytes 8704 | tf_op jit(solution)/shard_map/scatter | solution.py:103
  26.1 8.6 %all-to-all-start.1 = ((bf16[32,1,128]{2,1,0:T(2,128)(2,1)}), bf16[32,1,128]{2,1,0:T(2,128)(2,1)S(1)}, u32[]{:S(2)}, u32[]{:S(2)}) async-start(bf16[32,1,128]{2,1,0:T(2,128)(2,1)} %copy.13), calls=%async_computation.1 | async-start | bytes 32768 | tf_op jit(solution)/shard_map/all_to_all | solution.py:109
  34.7 8.8 %scatter_custom_fusion = s32[4096]{0:T(1024)} fusion(s32[2048]{0:T(1024)S(1)} %bitcast.128, s32[2048]{0:T(1024)} %param.17, s32[]{:T(128)} %copy.36), kind=kCustom, calls=%fused_computation.50 | custom fusion | bytes 16896 | tf_op jit(solution)/shard_map/scatter | solution.py:105
  43.5 7.4 %all-to-all-start = ((s32[32,1,128]{2,1,0:T(1,128)}), s32[32,1,128]{2,1,0:T(1,128)S(1)}, u32[]{:S(2)}, u32[]{:S(2)}) async-start(s32[32,1,128]{2,1,0:T(1,128)} %bitcast.9), calls=%async_computation | async-start | bytes 32768 | tf_op jit(solution)/shard_map/all_to_all | solution.py:111
  50.9 7.2 %scatter_custom_fusion.3 = bf16[4096,128]{1,0:T(8,128)(2,1)} fusion(s32[2048]{0:T(1024)S(1)} %bitcast.129, bf16[2048,128]{1,0:T(8,128)(2,1)} %param.14, bf16[]{:T(256)} %constant.39.clone.1), kind=kCustom, calls=%fused_computation.37 | custom fusion | bytes 1049088 | tf_op jit(solution)/shard_map/scatter | solution.py:101
  58.0 7.4 %all-to-all-start.2 = ((bf16[32,128,128]{2,1,0:T(8,128)(2,1)}), bf16[32,128,128]{2,1,0:T(8,128)(2,1)S(1)}, u32[]{:S(2)}, u32[]{:S(2)}) async-start(bf16[32,128,128]{2,1,0:T(8,128)(2,1)} %bitcast.14), calls=%async_computation.2 | async-start | bytes 2097152 | tf_op jit(solution)/shard_map/all_to_all | solution.py:108
  65.5 28.8 %scatter_custom_fusion.2 = f32[1024]{0:T(1024)S(1)} fusion(s32[4096]{0:T(1024)S(1)} %bitcast.124, f32[4096]{0:T(1024)S(1)} %bitcast.126, f32[]{:T(128)} %constant.33.clone.1), kind=kCustom, calls=%fused_computation.54 | custom fusion | flops 4096 | bytes 4100 | tf_op jit(solution)/shard_map/scatter-add | solution.py:122
  94.3 27.2 %scatter_custom_fusion.4 = f32[1024,128]{1,0:T(8,128)S(1)} fusion(s32[4096]{0:T(1024)S(1)} %bitcast.125, bf16[4096,128]{1,0:T(8,128)(2,1)S(1)} %bitcast.103, f32[]{:T(128)} %constant.33.clone.1), kind=kCustom, calls=%fused_computation.13 | custom fusion | flops 1048576 | bytes 1572868 | tf_op jit(solution)/shard_map/scatter-add | solution.py:115
  125.2 142.5 %while.32 = (s32[]{:T(128)}, f32[1,1024,128]{2,1,0:T(8,128)S(1)}, f32[1,1024]{1,0:T(1,128)S(1)}, s32[]{:T(128)}) while((s32[]{:T(128)}, f32[1,1024,128]{2,1,0:T(8,128)S(1)}, f32[1,1024]{1,0:T(1,128)S(1)}, s32[]{:T(128)}) %tuple.70), condition=%wide.region_11.12_spmd, body=%wide.region_10.11_spmd.sunk | while | flops 655362 | bytes 6295685 | solution.py:131
  129.6 3.7 collective-permute-done.1
  133.3 4.4 collective-permute-done
  146.0 5.0 collective-permute-done
  159.4 4.4 collective-permute-done
  172.2 5.9 collective-permute-done
  186.5 6.5 collective-permute-done
  201.3 6.5 collective-permute-done
  216.2 6.5 collective-permute-done
  231.1 6.5 collective-permute-done
  246.0 6.5 collective-permute-done
  260.9 6.5 collective-permute-done
  267.7 10.0 %while.33 = (s32[]{:T(128)}, f32[1,1024,128]{2,1,0:T(8,128)S(1)}, f32[128]{0:T(128)S(1)}, s32[]{:T(128)}) while((s32[]{:T(128)}, f32[1,1024,128]{2,1,0:T(8,128)S(1)}, f32[128]{0:T(128)S(1)}, s32[]{:T(128)}) %tuple.71), condition=%wide.region_13.14_spmd.clone, body=%wide.region_12.13_spmd.clone.sunk | while | flops 1180674 | bytes 6530101 | solution.py:66
  278.3 16.2 %psum.70 = f32[1024]{0:T(1024)S(1)} all-reduce(f32[1024]{0:T(1024)S(1)} %bitcast.123), channel_id=1, replica_groups=mesh['grp'=8,'tile'=32] {'grp'}, use_global_device_ids=true, to_apply=%region_14.15 | all-reduce | flops 1024 | bytes 8192 | tf_op jit(solution)/shard_map/psum | solution.py:74
  294.9 60.4 %psum.71 = f32[128]{0:T(128)S(1)} all-reduce(f32[128]{0:T(128)S(1)} %convolution_bitcast_fusion.4), channel_id=1, replica_groups=mesh['grp'=8,'tile'=32] {'tile'}, use_global_device_ids=true, to_apply=%region_15.16 | all-reduce | flops 128 | bytes 1024 | tf_op jit(solution)/shard_map/psum | solution.py:77
  356.0 10.7 %psum.72 = f32[1024]{0:T(1024)S(1)} all-reduce(f32[1024]{0:T(1024)S(1)} %bitcast.119), channel_id=1, replica_groups=mesh['grp'=8,'tile'=32] {'grp'}, use_global_device_ids=true, to_apply=%region_16.17 | all-reduce | flops 1024 | bytes 8192 | tf_op jit(solution)/shard_map/psum | solution.py:74
  367.1 68.3 %psum.73 = f32[128]{0:T(128)S(1)} all-reduce(f32[128]{0:T(128)S(1)} %convolution_bitcast_fusion.3), channel_id=1, replica_groups=mesh['grp'=8,'tile'=32] {'tile'}, use_global_device_ids=true, to_apply=%region_17.18 | all-reduce | flops 128 | bytes 1024 | tf_op jit(solution)/shard_map/psum | solution.py:77
  435.9 12.4 %psum.74 = f32[1024]{0:T(1024)S(1)} all-reduce(f32[1024]{0:T(1024)S(1)} %bitcast.120), channel_id=1, replica_groups=mesh['grp'=8,'tile'=32] {'grp'}, use_global_device_ids=true, to_apply=%region_18.19 | all-reduce | flops 1024 | bytes 8192 | tf_op jit(solution)/shard_map/psum | solution.py:74
  448.7 66.5 %psum.75 = f32[128]{0:T(128)S(1)} all-reduce(f32[128]{0:T(128)S(1)} %convolution_bitcast_fusion.2), channel_id=1, replica_groups=mesh['grp'=8,'tile'=32] {'tile'}, use_global_device_ids=true, to_apply=%region_19.20 | all-reduce | flops 128 | bytes 1024 | tf_op jit(solution)/shard_map/psum | solution.py:77
  515.8 10.7 %psum.76 = f32[1024]{0:T(1024)S(1)} all-reduce(f32[1024]{0:T(1024)S(1)} %bitcast.121), channel_id=1, replica_groups=mesh['grp'=8,'tile'=32] {'grp'}, use_global_device_ids=true, to_apply=%region_20.21 | all-reduce | flops 1024 | bytes 8192 | tf_op jit(solution)/shard_map/psum | solution.py:74
  526.9 66.2 %psum.77 = f32[128]{0:T(128)S(1)} all-reduce(f32[128]{0:T(128)S(1)} %convolution_bitcast_fusion.1), channel_id=1, replica_groups=mesh['grp'=8,'tile'=32] {'tile'}, use_global_device_ids=true, to_apply=%region_21.22 | all-reduce | flops 128 | bytes 1024 | tf_op jit(solution)/shard_map/psum | solution.py:77
  593.6 12.4 %psum.78 = f32[1024]{0:T(1024)S(1)} all-reduce(f32[1024]{0:T(1024)S(1)} %bitcast.122), channel_id=1, replica_groups=mesh['grp'=8,'tile'=32] {'grp'}, use_global_device_ids=true, to_apply=%region_22.23 | all-reduce | flops 1024 | bytes 8192 | tf_op jit(solution)/shard_map/psum | solution.py:74
  606.4 66.4 %psum.79 = f32[128]{0:T(128)S(1)} all-reduce(f32[128]{0:T(128)S(1)} %convolution_bitcast_fusion), channel_id=1, replica_groups=mesh['grp'=8,'tile'=32] {'tile'}, use_global_device_ids=true, to_apply=%region_23.24 | all-reduce | flops 128 | bytes 1024 | tf_op jit(solution)/shard_map/psum | solution.py:77
  (140 shorter events, 104.8 us)
Async XLA Ops:
  0.0 10.6 %copy-start.2 = (s32[2048,1]{0,1:T(1,128)S(1)}, s32[2048,1]{0,1:T(1,128)}, u32[]{:S(2)}) copy-start(s32[2048,1]{0,1:T(1,128)} %param.16) | copy-start | bytes 24580
  26.1 17.4 %all-to-all-start.1 = ((bf16[32,1,128]{2,1,0:T(2,128)(2,1)}), bf16[32,1,128]{2,1,0:T(2,128)(2,1)S(1)}, u32[]{:S(2)}, u32[]{:S(2)}) async-start(bf16[32,1,128]{2,1,0:T(2,128)(2,1)} %copy.13), calls=%async_computation.1 | async-start | bytes 32768 | tf_op jit(solution)/shard_map/all_to_all | solution.py:109
  43.5 14.6 %all-to-all-start = ((s32[32,1,128]{2,1,0:T(1,128)}), s32[32,1,128]{2,1,0:T(1,128)S(1)}, u32[]{:S(2)}, u32[]{:S(2)}) async-start(s32[32,1,128]{2,1,0:T(1,128)} %bitcast.9), calls=%async_computation | async-start | bytes 32768 | tf_op jit(solution)/shard_map/all_to_all | solution.py:111
  58.0 36.2 %all-to-all-start.2 = ((bf16[32,128,128]{2,1,0:T(8,128)(2,1)}), bf16[32,128,128]{2,1,0:T(8,128)(2,1)S(1)}, u32[]{:S(2)}, u32[]{:S(2)}) async-start(bf16[32,128,128]{2,1,0:T(8,128)(2,1)} %bitcast.14), calls=%async_computation.2 | async-start | bytes 2097152 | tf_op jit(solution)/shard_map/all_to_all | solution.py:108
  65.4 56.1 %copy-start = (f32[1,1024]{1,0:T(1,128)S(1)}, f32[1,1024]{1,0:T(1,128)}, u32[]{:S(2)}) copy-start(f32[1,1024]{1,0:T(1,128)} %param.18) | copy-start | bytes 12292
  121.5 3.7 copy-start.1
  125.2 142.5 %copy-start.3 = (f32[128]{0:T(128)S(1)}, f32[128]{0:T(128)}, u32[]{:S(2)}) copy-start(f32[128]{0:T(128)} %param.20) | copy-start | bytes 1540
  125.2 8.0 %collective-permute-start.1 = (f32[1,1024,128]{2,1,0:T(8,128)S(1)}, f32[1,1024,128]{2,1,0:T(8,128)S(1)}, u32[]{:S(2)}, u32[]{:S(2)}) collective-permute-start(f32[1,1024,128]{2,1,0:T(8,128)S(1)} %get-tuple-element.194), channel_id=1, source_target_pairs={{0,1},{1,2},{2,3},{3,4},{4,5},{5,6},{6,7},{7,8},{8,9},{9,10},{10,1... | collective-permute-start | bytes 1572872 | tf_op jit(solution)/shard_map/while/body/eval_jaxpr/ppermute | solution.py:22
  127.2 10.5 %collective-permute-start = (f32[1,1024,128]{2,1,0:T(8,128)S(1)}, f32[1,1024,128]{2,1,0:T(8,128)S(1)}, u32[]{:S(2)}, u32[]{:S(2)}) collective-permute-start(f32[1,1024,128]{2,1,0:T(8,128)S(1)} %get-tuple-element.194), channel_id=1, source_target_pairs={{1,0},{2,1},{3,2},{4,3},{5,4},{6,5},{7,6},{8,7},{9,8},{10,9},{11,1... | collective-permute-start | bytes 1572872 | tf_op jit(solution)/shard_map/while/body/eval_jaxpr/ppermute | solution.py:24
  138.0 8.0 %collective-permute-start.1 = (f32[1,1024,128]{2,1,0:T(8,128)S(1)}, f32[1,1024,128]{2,1,0:T(8,128)S(1)}, u32[]{:S(2)}, u32[]{:S(2)}) collective-permute-start(f32[1,1024,128]{2,1,0:T(8,128)S(1)} %get-tuple-element.194), channel_id=1, source_target_pairs={{0,1},{1,2},{2,3},{3,4},{4,5},{5,6},{6,7},{7,8},{8,9},{9,10},{10,1... | collective-permute-start | bytes 1572872 | tf_op jit(solution)/shard_map/while/body/eval_jaxpr/ppermute | solution.py:22
  139.9 11.1 %collective-permute-start = (f32[1,1024,128]{2,1,0:T(8,128)S(1)}, f32[1,1024,128]{2,1,0:T(8,128)S(1)}, u32[]{:S(2)}, u32[]{:S(2)}) collective-permute-start(f32[1,1024,128]{2,1,0:T(8,128)S(1)} %get-tuple-element.194), channel_id=1, source_target_pairs={{1,0},{2,1},{3,2},{4,3},{5,4},{6,5},{7,6},{8,7},{9,8},{10,9},{11,1... | collective-permute-start | bytes 1572872 | tf_op jit(solution)/shard_map/while/body/eval_jaxpr/ppermute | solution.py:24
  151.4 8.0 %collective-permute-start.1 = (f32[1,1024,128]{2,1,0:T(8,128)S(1)}, f32[1,1024,128]{2,1,0:T(8,128)S(1)}, u32[]{:S(2)}, u32[]{:S(2)}) collective-permute-start(f32[1,1024,128]{2,1,0:T(8,128)S(1)} %get-tuple-element.194), channel_id=1, source_target_pairs={{0,1},{1,2},{2,3},{3,4},{4,5},{5,6},{6,7},{7,8},{8,9},{9,10},{10,1... | collective-permute-start | bytes 1572872 | tf_op jit(solution)/shard_map/while/body/eval_jaxpr/ppermute | solution.py:22
  153.3 10.5 %collective-permute-start = (f32[1,1024,128]{2,1,0:T(8,128)S(1)}, f32[1,1024,128]{2,1,0:T(8,128)S(1)}, u32[]{:S(2)}, u32[]{:S(2)}) collective-permute-start(f32[1,1024,128]{2,1,0:T(8,128)S(1)} %get-tuple-element.194), channel_id=1, source_target_pairs={{1,0},{2,1},{3,2},{4,3},{5,4},{6,5},{7,6},{8,7},{9,8},{10,9},{11,1... | collective-permute-start | bytes 1572872 | tf_op jit(solution)/shard_map/while/body/eval_jaxpr/ppermute | solution.py:24
  164.2 8.0 %collective-permute-start.1 = (f32[1,1024,128]{2,1,0:T(8,128)S(1)}, f32[1,1024,128]{2,1,0:T(8,128)S(1)}, u32[]{:S(2)}, u32[]{:S(2)}) collective-permute-start(f32[1,1024,128]{2,1,0:T(8,128)S(1)} %get-tuple-element.194), channel_id=1, source_target_pairs={{0,1},{1,2},{2,3},{3,4},{4,5},{5,6},{6,7},{7,8},{8,9},{9,10},{10,1... | collective-permute-start | bytes 1572872 | tf_op jit(solution)/shard_map/while/body/eval_jaxpr/ppermute | solution.py:22
  166.1 12.0 %collective-permute-start = (f32[1,1024,128]{2,1,0:T(8,128)S(1)}, f32[1,1024,128]{2,1,0:T(8,128)S(1)}, u32[]{:S(2)}, u32[]{:S(2)}) collective-permute-start(f32[1,1024,128]{2,1,0:T(8,128)S(1)} %get-tuple-element.194), channel_id=1, source_target_pairs={{1,0},{2,1},{3,2},{4,3},{5,4},{6,5},{7,6},{8,7},{9,8},{10,9},{11,1... | collective-permute-start | bytes 1572872 | tf_op jit(solution)/shard_map/while/body/eval_jaxpr/ppermute | solution.py:24
  178.4 8.0 %collective-permute-start.1 = (f32[1,1024,128]{2,1,0:T(8,128)S(1)}, f32[1,1024,128]{2,1,0:T(8,128)S(1)}, u32[]{:S(2)}, u32[]{:S(2)}) collective-permute-start(f32[1,1024,128]{2,1,0:T(8,128)S(1)} %get-tuple-element.194), channel_id=1, source_target_pairs={{0,1},{1,2},{2,3},{3,4},{4,5},{5,6},{6,7},{7,8},{8,9},{9,10},{10,1... | collective-permute-start | bytes 1572872 | tf_op jit(solution)/shard_map/while/body/eval_jaxpr/ppermute | solution.py:22
  180.4 12.6 %collective-permute-start = (f32[1,1024,128]{2,1,0:T(8,128)S(1)}, f32[1,1024,128]{2,1,0:T(8,128)S(1)}, u32[]{:S(2)}, u32[]{:S(2)}) collective-permute-start(f32[1,1024,128]{2,1,0:T(8,128)S(1)} %get-tuple-element.194), channel_id=1, source_target_pairs={{1,0},{2,1},{3,2},{4,3},{5,4},{6,5},{7,6},{8,7},{9,8},{10,9},{11,1... | collective-permute-start | bytes 1572872 | tf_op jit(solution)/shard_map/while/body/eval_jaxpr/ppermute | solution.py:24
  193.3 8.0 %collective-permute-start.1 = (f32[1,1024,128]{2,1,0:T(8,128)S(1)}, f32[1,1024,128]{2,1,0:T(8,128)S(1)}, u32[]{:S(2)}, u32[]{:S(2)}) collective-permute-start(f32[1,1024,128]{2,1,0:T(8,128)S(1)} %get-tuple-element.194), channel_id=1, source_target_pairs={{0,1},{1,2},{2,3},{3,4},{4,5},{5,6},{6,7},{7,8},{8,9},{9,10},{10,1... | collective-permute-start | bytes 1572872 | tf_op jit(solution)/shard_map/while/body/eval_jaxpr/ppermute | solution.py:22
  195.2 12.6 %collective-permute-start = (f32[1,1024,128]{2,1,0:T(8,128)S(1)}, f32[1,1024,128]{2,1,0:T(8,128)S(1)}, u32[]{:S(2)}, u32[]{:S(2)}) collective-permute-start(f32[1,1024,128]{2,1,0:T(8,128)S(1)} %get-tuple-element.194), channel_id=1, source_target_pairs={{1,0},{2,1},{3,2},{4,3},{5,4},{6,5},{7,6},{8,7},{9,8},{10,9},{11,1... | collective-permute-start | bytes 1572872 | tf_op jit(solution)/shard_map/while/body/eval_jaxpr/ppermute | solution.py:24
  208.2 8.0 %collective-permute-start.1 = (f32[1,1024,128]{2,1,0:T(8,128)S(1)}, f32[1,1024,128]{2,1,0:T(8,128)S(1)}, u32[]{:S(2)}, u32[]{:S(2)}) collective-permute-start(f32[1,1024,128]{2,1,0:T(8,128)S(1)} %get-tuple-element.194), channel_id=1, source_target_pairs={{0,1},{1,2},{2,3},{3,4},{4,5},{5,6},{6,7},{7,8},{8,9},{9,10},{10,1... | collective-permute-start | bytes 1572872 | tf_op jit(solution)/shard_map/while/body/eval_jaxpr/ppermute | solution.py:22
  210.1 12.6 %collective-permute-start = (f32[1,1024,128]{2,1,0:T(8,128)S(1)}, f32[1,1024,128]{2,1,0:T(8,128)S(1)}, u32[]{:S(2)}, u32[]{:S(2)}) collective-permute-start(f32[1,1024,128]{2,1,0:T(8,128)S(1)} %get-tuple-element.194), channel_id=1, source_target_pairs={{1,0},{2,1},{3,2},{4,3},{5,4},{6,5},{7,6},{8,7},{9,8},{10,9},{11,1... | collective-permute-start | bytes 1572872 | tf_op jit(solution)/shard_map/while/body/eval_jaxpr/ppermute | solution.py:24
  223.1 8.0 %collective-permute-start.1 = (f32[1,1024,128]{2,1,0:T(8,128)S(1)}, f32[1,1024,128]{2,1,0:T(8,128)S(1)}, u32[]{:S(2)}, u32[]{:S(2)}) collective-permute-start(f32[1,1024,128]{2,1,0:T(8,128)S(1)} %get-tuple-element.194), channel_id=1, source_target_pairs={{0,1},{1,2},{2,3},{3,4},{4,5},{5,6},{6,7},{7,8},{8,9},{9,10},{10,1... | collective-permute-start | bytes 1572872 | tf_op jit(solution)/shard_map/while/body/eval_jaxpr/ppermute | solution.py:22
  225.0 12.6 %collective-permute-start = (f32[1,1024,128]{2,1,0:T(8,128)S(1)}, f32[1,1024,128]{2,1,0:T(8,128)S(1)}, u32[]{:S(2)}, u32[]{:S(2)}) collective-permute-start(f32[1,1024,128]{2,1,0:T(8,128)S(1)} %get-tuple-element.194), channel_id=1, source_target_pairs={{1,0},{2,1},{3,2},{4,3},{5,4},{6,5},{7,6},{8,7},{9,8},{10,9},{11,1... | collective-permute-start | bytes 1572872 | tf_op jit(solution)/shard_map/while/body/eval_jaxpr/ppermute | solution.py:24
  237.9 8.0 %collective-permute-start.1 = (f32[1,1024,128]{2,1,0:T(8,128)S(1)}, f32[1,1024,128]{2,1,0:T(8,128)S(1)}, u32[]{:S(2)}, u32[]{:S(2)}) collective-permute-start(f32[1,1024,128]{2,1,0:T(8,128)S(1)} %get-tuple-element.194), channel_id=1, source_target_pairs={{0,1},{1,2},{2,3},{3,4},{4,5},{5,6},{6,7},{7,8},{8,9},{9,10},{10,1... | collective-permute-start | bytes 1572872 | tf_op jit(solution)/shard_map/while/body/eval_jaxpr/ppermute | solution.py:22
  239.9 12.6 %collective-permute-start = (f32[1,1024,128]{2,1,0:T(8,128)S(1)}, f32[1,1024,128]{2,1,0:T(8,128)S(1)}, u32[]{:S(2)}, u32[]{:S(2)}) collective-permute-start(f32[1,1024,128]{2,1,0:T(8,128)S(1)} %get-tuple-element.194), channel_id=1, source_target_pairs={{1,0},{2,1},{3,2},{4,3},{5,4},{6,5},{7,6},{8,7},{9,8},{10,9},{11,1... | collective-permute-start | bytes 1572872 | tf_op jit(solution)/shard_map/while/body/eval_jaxpr/ppermute | solution.py:24
  252.8 8.0 %collective-permute-start.1 = (f32[1,1024,128]{2,1,0:T(8,128)S(1)}, f32[1,1024,128]{2,1,0:T(8,128)S(1)}, u32[]{:S(2)}, u32[]{:S(2)}) collective-permute-start(f32[1,1024,128]{2,1,0:T(8,128)S(1)} %get-tuple-element.194), channel_id=1, source_target_pairs={{0,1},{1,2},{2,3},{3,4},{4,5},{5,6},{6,7},{7,8},{8,9},{9,10},{10,1... | collective-permute-start | bytes 1572872 | tf_op jit(solution)/shard_map/while/body/eval_jaxpr/ppermute | solution.py:22
  254.8 12.6 %collective-permute-start = (f32[1,1024,128]{2,1,0:T(8,128)S(1)}, f32[1,1024,128]{2,1,0:T(8,128)S(1)}, u32[]{:S(2)}, u32[]{:S(2)}) collective-permute-start(f32[1,1024,128]{2,1,0:T(8,128)S(1)} %get-tuple-element.194), channel_id=1, source_target_pairs={{1,0},{2,1},{3,2},{4,3},{5,4},{6,5},{7,6},{8,7},{9,8},{10,9},{11,1... | collective-permute-start | bytes 1572872 | tf_op jit(solution)/shard_map/while/body/eval_jaxpr/ppermute | solution.py:24
  277.7 77.7 %copy-start.4 = (f32[128]{0:T(128)S(1)}, f32[128]{0:T(128)}, u32[]{:S(2)}) copy-start(f32[128]{0:T(128)} %param.21) | copy-start | bytes 1540
where the time goes:
time: 675 us; the launch traced here: 674 us
  blocking collectives  390 us (58%)
  waiting for transfers between devices  95.3 us (14%)
  other arithmetic  79 us (12%)
  starting transfers between devices  66.9 us (10%)
  local copies, waits for them, and re-layouts  36.5 us (5%)
    psum x5, blocking collectives, scale_plan(): col_sums = lax.psum(partial_cols, 'tile')  328 us
    psum x5, blocking collectives, scale_plan(): row_sums = lax.psum(partial_rows, 'grp')  62.4 us
    ppermute x10, waiting for transfers between devices, padded_2(): lax.ppermute(head, axis, [((i + 1) % count, i) for i in range(ends)])  58.7 us
    ppermute x10, waiting for transfers between devices, padded_2(): lax.ppermute(tail, axis, [(i, (i + 1) % count) for i in range(ends)])  36.6 us
    scatter-add x1, other arithmetic, body(): cell_mass = jnp.zeros((cells_local,), jnp.float32).at[flat_cell].add(got_...  28.8 us
    scatter-add x1, other arithmetic, body(): plan_field.at[flat_cell]  27.2 us
    ppermute x10, starting transfers between devices, padded_2(): lax.ppermute(head, axis, [((i + 1) % count, i) for i in range(ends)])  24.3 us
    ppermute x10, starting transfers between devices, padded_2(): lax.ppermute(tail, axis, [(i, (i + 1) % count) for i in range(ends)])  19.2 us
  transfers between devices with their start and end apart: 23, of which 20 were waited for; matrix products, arithmetic and copies ran while one was open for 7% of the time, Pallas kernels for 0%

commit v1 on v0

v1 whole, which is shorter than its diff:
```python
import functools

import jax
import jax.numpy as jnp
from jax import lax
from jax.experimental import pallas as pl
from jax.experimental.pallas import tpu as pltpu
from jax.sharding import PartitionSpec as P

PATCH_ROW = 32
HEAT_STEPS = 10
SCALING_ROUNDS = 5
EXPONENT_GAIN = 2.0
LANES = 128
CAP = 128
META = 16
F32 = jnp.float32
BF16 = jnp.bfloat16
NT = (((1,), (1,)), ((), ()))
EXACT = lax.Precision.HIGHEST


def iota(shape, axis):
    return lax.broadcasted_iota(jnp.int32, shape, axis)


def call(kernel, out_shape, operands, scratch=(), hbm=(), out_hbm=False):
    specs = []
    for i in range(len(operands)):
        space = pltpu.HBM if i in hbm else pltpu.VMEM
        specs.append(pl.BlockSpec(memory_space=space))
    out_space = pltpu.HBM if out_hbm else pltpu.VMEM
    outs = jax.tree.map(lambda _: pl.BlockSpec(memory_space=out_space), out_shape)
    return pl.pallas_call(
        kernel,
        out_shape=out_shape,
        in_specs=specs,
        out_specs=outs,
        scratch_shapes=list(scratch),
        compiler_params=pltpu.CompilerParams(vmem_limit_bytes=(60 if hbm else 40) * 2**20),
    )(*operands)


def onehot_rows(index, base, rows):
    n = index.shape[1]
    local = jnp.clip(index - float(base), -1.0, float(rows))
    local = jnp.broadcast_to(local, (16, n)).astype(BF16)
    row = iota((rows, LANES), 0).astype(F32).astype(BF16)
    row = row.reshape(rows // 16, 16, LANES)
    one = jnp.ones((rows // 16, 16, LANES), BF16)
    zero = jnp.zeros((rows // 16, 16, LANES), BF16)
    pieces = []
    for j in range(n // LANES):
        piece = local[None, :, j * LANES : (j + 1) * LANES]
        piece = jnp.broadcast_to(piece, row.shape)
        pieces.append(jnp.where(row == piece, one, zero).reshape(rows, LANES))
    return jnp.concatenate(pieces, axis=1)


def pack_kernel(
    owner_hbm, cell_hbm, weight_hbm, terms_hbm, out_hbm,
    out_ref, onehot_ref, owner_ref, cell_ref, weight_ref, terms_ref, sems, out_sems,
):
    tiles = out_ref.shape[0]
    spots = terms_ref.shape[0]
    block = 256
    pairs = [
        (owner_hbm, owner_ref), (cell_hbm, cell_ref), (weight_hbm, weight_ref), (terms_hbm, terms_ref),
    ]
    copies = [pltpu.make_async_copy(src, dst, sems.at[i]) for i, (src, dst) in enumerate(pairs)]
    for copy in copies:
        copy.start()
    before = (iota((block, block), 0) < iota((block, block), 1)).astype(F32).astype(BF16)
    copies[0].wait()
    owner = owner_ref[...]
    base = jnp.zeros((tiles, 1), F32)
    ranks = []
    for b in range(spots // block):
        own = owner[:, b * block : (b + 1) * block]
        member = (iota((tiles, block), 0) == own).astype(F32)
        inside = jnp.dot(member.astype(BF16), before, preferred_element_type=F32)
        ranks.append(jnp.sum(member * (inside + base), axis=0, keepdims=True))
        base = base + inside[:, block - 1 : block] + member[:, block - 1 : block]
    rank = jnp.concatenate(ranks, axis=1)
    slot = owner.astype(F32) * float(CAP) + rank
    for copy in copies[1:]:
        copy.wait()
    cell = cell_ref[...]
    high = (cell // 32).astype(F32)
    low = (cell % 32).astype(F32)
    weight = weight_ref[...].astype(F32)
    weight = jnp.concatenate([weight[i : i + 1] for i in range(spots // LANES)], axis=1)
    which = iota((tiles * 8, spots), 0)
    kind = which % 8
    value = jnp.where(kind == 0, weight, jnp.where(kind == 1, high, jnp.where(kind == 2, low, 0.0)))
    value = jnp.where(which // 8 == owner, value, 0.0).astype(BF16)
    onehot_ref[1, 0:CAP, :] = onehot_rows(rank, 0, CAP)
    meta = lax.dot_general(value, onehot_ref[1, 0:CAP, :], NT, preferred_element_type=F32)
    empty = jnp.zeros((8, LANES), F32)
    for t in range(tiles):
        out_ref[t, CAP : CAP + META, :] = jnp.concatenate(
            [meta[8 * t : 8 * t + 8], empty], axis=0
        ).astype(BF16)
    terms = terms_ref[...]
    leaving = []
    for chunk in range(tiles * CAP // 256):
        onehot_ref[chunk % 2] = onehot_rows(slot, chunk * 256, 256)
        rows = jnp.dot(onehot_ref[chunk % 2], terms, preferred_element_type=F32).astype(BF16)
        out_ref[2 * chunk, 0:CAP, :] = rows[:CAP]
        out_ref[2 * chunk + 1, 0:CAP, :] = rows[CAP:]
        both = pl.ds(2 * chunk, 2)
        leaving.append(
            pltpu.make_async_copy(out_ref.at[both], out_hbm.at[both], out_sems.at[chunk])
        )
        leaving[-1].start()
    for copy in leaving:
        copy.wait()


def column_of(row):
    return jnp.broadcast_to(row, (LANES, LANES)).T


def prep_kernel(col_ref, tgt_ref, ccol_ref, patch_ref):
    for t in range(col_ref.shape[1] // LANES):
        ccol_ref[t * LANES : (t + 1) * LANES, :] = column_of(
            col_ref[:, t * LANES : (t + 1) * LANES]
        )
    coef = column_of(tgt_ref[...])
    place = iota((LANES, LANES), 0)
    field = (place == iota((LANES, LANES), 1)).astype(F32)
    first = place % PATCH_ROW == 0
    last = place % PATCH_ROW == PATCH_ROW - 1
    zeros = jnp.zeros((PATCH_ROW, LANES), F32)
    for _ in range(HEAT_STEPS):
        west = jnp.where(first, 0.0, pltpu.roll(field, 1, 0))
        east = jnp.where(last, 0.0, pltpu.roll(field, LANES - 1, 0))
        north = jnp.concatenate([zeros, field[: LANES - PATCH_ROW]], axis=0)
        south = jnp.concatenate([field[PATCH_ROW:], zeros], axis=0)
        field = field + coef * (west + east + north + south - 4.0 * field)
    patch_ref[...] = field


def gather_kernel(msg_ref, ccol_ref, rcoef_ref, out_ref, onehot_ref, a_ref, b_ref):
    tiles = msg_ref.shape[0]
    cells = ccol_ref.shape[0]
    meta = msg_ref[:, CAP : CAP + META, :].astype(F32)
    weight = jnp.concatenate([meta[t, 0:1, :] for t in range(tiles)], axis=1)
    high = jnp.concatenate([meta[t, 1:2, :] for t in range(tiles)], axis=1)
    low = jnp.concatenate([meta[t, 2:3, :] for t in range(tiles)], axis=1)
    cell = high * 32.0 + low
    slots = tiles * CAP
    rows = msg_ref[:, 0:CAP, :].reshape(slots, LANES)
    pad = jnp.zeros((8, LANES), F32)
    for ref in (a_ref, b_ref):
        ref[0:8, :] = pad
        ref[8 + cells : 16 + cells, :] = pad
    for chunk in range(cells // 256):
        onehot_ref[chunk % 2] = onehot_rows(cell, chunk * 256, 256)
        a_ref[8 + 256 * chunk : 8 + 256 * (chunk + 1), :] = jnp.dot(
            onehot_ref[chunk % 2], rows, preferred_element_type=F32
        )
    blocks = cells // PATCH_ROW
    lane_shift = (lax.rem(lax.axis_index("tile"), 4) * 32).astype(F32)
    upper = jnp.where(iota((blocks, slots), 0).astype(F32) == high, weight, 0.0).astype(BF16)
    lower = (iota((LANES, slots), 0).astype(F32) == low + lane_shift).astype(F32).astype(BF16)
    mass = lax.dot_general(upper, lower, NT, preferred_element_type=F32)

    def heated(src, c, size):
        o = 8 + c * size
        mid = src[o : o + size, :]
        beside = src[o - 1 : o - 1 + size, :] + src[o + 1 : o + 1 + size, :]
        coef = ccol_ref[c * size : (c + 1) * size, :]
        return mid + coef * (beside - 2.0 * mid)

    def step(src, dst):
        size = 128
        for c in range(cells // size):
            dst[8 + c * size : 8 + (c + 1) * size, :] = heated(src, c, size)

    def two_steps(_, carry):
        step(a_ref, b_ref)
        step(b_ref, a_ref)
        return carry

    lax.fori_loop(0, HEAT_STEPS // 2 - 1, two_steps, 0)
    step(a_ref, b_ref)
    sub = iota((8, LANES), 0)
    for d in range(tiles):
        out_ref[d, 0:32, :] = heated(b_ref, d, 32)
        out_ref[d, 32:40, :] = jnp.where(
            sub == 0, rcoef_ref[d : d + 1, :], jnp.where(sub == 1, mass[d : d + 1, :], 0.0)
        )


def tile_of(parts):
    sub = iota((8, LANES), 0)
    out = jnp.broadcast_to(parts[0], (8, LANES))
    for t in range(1, 8):
        out = jnp.where(sub == t, parts[t], out)
    return out


def row_partials(kt_ref, vcol):
    parts = []
    for t in range(8):
        piece = kt_ref[:, t * LANES : (t + 1) * LANES].astype(F32)
        if vcol is not None:
            piece = piece * vcol
        parts.append(jnp.sum(piece, axis=0, keepdims=True))
    return tile_of(parts)


def band_kernel(
    msg_ref, patch_ref, weight_ref, kt_ref, short_ref, mass_ref, out_ref, coef_ref, field_ref
):
    tiles = msg_ref.shape[0]
    sub = iota((8, LANES), 0)
    mass = jnp.zeros((8, LANES), F32)
    coef = []
    for r in range(tiles):
        mass = mass + jnp.where(sub == r // 4, msg_ref[r, 33:34, :], 0.0)
    mass_ref[...] = mass
    for b in range(tiles // 8):
        coef.append(tile_of([msg_ref[8 * b + r, 32:33, :] for r in range(8)]))
    coef.append(jnp.zeros((LANES - tiles, LANES), F32))
    coef = jnp.concatenate(coef, axis=0).T
    for r in range(tiles):
        coef_ref[r, :, :] = jnp.broadcast_to(coef[0:32, r : r + 1], (32, LANES))
    zero = jnp.zeros((8, LANES), F32)
    for b in range(4):
        place = slice(8 * b, 8 * b + 8)

        def step(_, field):
            out = []
            for r in range(tiles):
                up = field[r - 1] if r > 0 else zero
                down = field[r + 1] if r < tiles - 1 else zero
                out.append(field[r] + coef_ref[r, place, :] * (up + down - 2.0 * field[r]))
            return tuple(out)

        field = lax.fori_loop(
            0, HEAT_STEPS, step, tuple(msg_ref[r, place, :] for r in range(tiles))
        )
        for r in range(tiles):
            field_ref[32 * r + 8 * b : 32 * r + 8 * b + 8, :] = field[r]
    smooth = lax.dot_general(
        patch_ref[...], field_ref[...], NT, preferred_element_type=F32, precision=EXACT
    )
    kernel = jnp.exp(EXPONENT_GAIN * smooth)
    kt_ref[...] = kernel
    short_ref[...] = kernel.astype(BF16)
    tile = row_partials(kt_ref, None)
    for g in range(out_ref.shape[0]):
        out_ref[g, 0:8, :] = tile
        out_ref[g, 8:16, :] = jnp.broadcast_to(weight_ref[...], (8, LANES))


def row_scale(msg_ref, mass_ref):
    total = msg_ref[0, 0:8, :]
    for g in range(1, msg_ref.shape[0]):
        total = total + msg_ref[g, 0:8, :]
    return mass_ref[...] / total


def scaled_columns(kt_ref, scale):
    pieces = [kt_ref[:, t * LANES : (t + 1) * LANES].astype(F32) for t in range(8)]
    return [piece * scale[t : t + 1, :] for t, piece in enumerate(pieces)]


def column_partials(kt_ref, scale):
    total = functools.reduce(lambda a, b: a + b, scaled_columns(kt_ref, scale))
    return jnp.sum(total.T, axis=0, keepdims=True)


def by_distance(msg_ref):
    groups = msg_ref.shape[0]
    me = lax.axis_index("grp")
    return tile_of([msg_ref[lax.rem(me + groups - k, groups), 8:9, :] for k in range(groups)])


def row_kernel(msg_ref, mass_ref, kt_ref, out_ref, weights_ref):
    weights_ref[...] = by_distance(msg_ref)
    column = column_partials(kt_ref, row_scale(msg_ref, mass_ref))
    for t in range(out_ref.shape[0]):
        out_ref[t, :, :] = column


def send_wide(out_ref, kernel_refs, scale):
    tile = tile_of([column_partials(ref, scale) for ref in kernel_refs])
    for t in range(out_ref.shape[0]):
        out_ref[t, :, :] = tile


def choose_kernel(even_ref, odd_ref, out_ref):
    odd = lax.rem(lax.axis_index("tile"), 2)

    @pl.when(odd == 0)
    def _():
        out_ref[...] = even_ref[...]

    @pl.when(odd == 1)
    def _():
        out_ref[...] = odd_ref[...]


def wide_row_sums(scale, kernel_refs):
    total = jnp.zeros((8, LANES), F32)
    for k, ref in enumerate(kernel_refs):
        total = total + row_partials(ref, column_of(scale[k : k + 1, :]))
    return total


def wide_row_kernel(msg_ref, mass_ref, *refs):
    kernel_refs, out_ref, later_ref = refs[:-2], refs[-2], refs[-1]
    scale = row_scale(msg_ref, mass_ref)
    send_wide(out_ref, kernel_refs, scale)
    later_ref[...] = scale * wide_row_sums(by_distance(msg_ref), kernel_refs)


def wide_row_scale(msg_ref, later_ref, weights_ref, kernel_refs):
    scale = column_scale([msg_ref[t] for t in range(msg_ref.shape[0])], weights_ref[...])
    return later_ref[...] / wide_row_sums(scale, kernel_refs)


def wide_round_kernel(msg_ref, later_ref, weights_ref, *refs):
    scale = wide_row_scale(msg_ref, later_ref, weights_ref, refs[:-1])
    send_wide(refs[-1], refs[:-1], scale)


def column_scale(parts, weight):
    while len(parts) > 1:
        parts = [a + b for a, b in zip(parts[0::2], parts[1::2])]
    return weight / parts[0]


def column_kernel(msg_ref, weight_ref, kt_ref, out_ref):
    scale = column_scale([msg_ref[t] for t in range(msg_ref.shape[0])], weight_ref[...])
    tile = row_partials(kt_ref, column_of(scale))
    for g in range(out_ref.shape[0]):
        out_ref[g, 0:8, :] = tile
        out_ref[g, 8:16, :] = jnp.broadcast_to(scale, (8, LANES))


def last_round_kernel(msg_ref, later_ref, weights_ref, *refs):
    out_ref = refs[-1]
    scale = wide_row_scale(msg_ref, later_ref, weights_ref, refs[:-1])
    pieces = scaled_columns(refs[0], scale)
    column = jnp.zeros((1, LANES), F32)
    for t in range(8):
        turned = pieces[t].T
        column = column + jnp.sum(turned, axis=0, keepdims=True)
        for r in range(4):
            out_ref[4 * t + r, 0:32, :] = turned[32 * r : 32 * r + 32]
    for r in range(out_ref.shape[0]):
        out_ref[r, 32:40, :] = jnp.broadcast_to(column, (8, LANES))


def plan_kernel(cell_count, msg_ref, weight_ref, out_hbm, plan_ref, sems):
    tiles = msg_ref.shape[0]
    scale = column_scale([msg_ref[t, 32:33, :] for t in range(tiles)], weight_ref[...])
    scale = scale * cell_count
    copies = []
    for d in range(tiles):
        plan_ref[0, 32 * d : 32 * d + 32, :] = msg_ref[d, 0:32, :] * scale
        if d % 8 == 7:
            rows = pl.ds(32 * (d - 7), 256)
            copies.append(
                pltpu.make_async_copy(
                    plan_ref.at[:, rows], out_hbm.at[:, rows], sems.at[d // 8]
                )
            )
            copies[-1].start()
    for copy in copies:
        copy.wait()


def swap(values, axis):
    return lax.all_to_all(values, axis, split_axis=0, concat_axis=0, tiled=True)


def body(spot_terms, spot_weight, spot_owner, spot_cell, col_coef, row_coef, tgt_coef, tgt_weight):
    tiles = lax.axis_size("tile")
    groups = lax.axis_size("grp")
    spots, columns = spot_terms.shape
    cells = col_coef.shape[1]
    shape = jax.ShapeDtypeStruct
    weight = tgt_weight.reshape(1, columns)

    packed = call(
        pack_kernel,
        shape((tiles, CAP + META, columns), BF16),
        [
            spot_owner.reshape(1, spots),
            spot_cell.reshape(1, spots),
            spot_weight.reshape(spots // LANES, LANES),
            spot_terms,
        ],
        scratch=[
            pltpu.VMEM((tiles, CAP + META, columns), BF16),
            pltpu.VMEM((2, 256, spots), BF16),
            pltpu.VMEM((1, spots), jnp.int32),
            pltpu.VMEM((1, spots), jnp.int32),
            pltpu.VMEM((spots // LANES, LANES), BF16),
            pltpu.VMEM((spots, columns), BF16),
            pltpu.SemaphoreType.DMA((4,)),
            pltpu.SemaphoreType.DMA((tiles * CAP // 256,)),
        ],
        hbm=(0, 1, 2, 3),
        out_hbm=True,
    )
    ccol, patch = call(
        prep_kernel,
        (shape((cells, LANES), F32), shape((LANES, LANES), F32)),
        [col_coef, tgt_coef.reshape(1, columns)],
    )
    rcoef = jnp.pad(row_coef.reshape(tiles, 32), ((0, 0), (0, LANES - 32)))
    got = swap(packed, "tile")
    sorted_field = call(
        gather_kernel,
        shape((tiles, 40, LANES), F32),
        [got, ccol, rcoef],
        scratch=[
            pltpu.VMEM((2, 256, tiles * CAP), BF16),
            pltpu.VMEM((cells + 16, LANES), F32),
            pltpu.VMEM((cells + 16, LANES), F32),
        ],
    )
    band = swap(sorted_field, "tile")
    tile = shape((8, LANES), F32)
    wide = shape((tiles, groups, LANES), F32)
    field = (columns, cells)
    kt, short, mass, rows = call(
        band_kernel,
        (shape(field, F32), shape(field, BF16), tile, shape((groups, 16, LANES), F32)),
        [band, patch, weight],
        scratch=[pltpu.VMEM((tiles, 32, LANES), F32), pltpu.VMEM((cells, LANES), F32)],
    )
    up = [(g, (g + 1) % groups) for g in range(groups)]
    down = [(g, (g - 1) % groups) for g in range(groups)]
    before = [kt, lax.ppermute(short, "grp", up)]
    after = [kt, lax.ppermute(short, "grp", down)]


    def forward(value):
        value, last, first = lax.optimization_barrier((value, before[-1], after[-1]))
        before[-1], after[-1] = last, first
        before.append(lax.ppermute(last, "grp", up))
        after.append(lax.ppermute(first, "grp", down))
        return value

    rows = forward(swap(rows, "grp"))
    leap = [
        (g * tiles + t, (g - 3 + 6 * (t % 2)) % groups * tiles + t)
        for g in range(groups)
        for t in range(tiles)
    ]
    opposite = call(choose_kernel, shape(field, BF16), [after[1], before[1]])
    opposite = lax.ppermute(opposite, ("grp", "tile"), leap)
    cols, weights = call(row_kernel, (shape((tiles, 1, LANES), F32), tile), [rows, mass, kt])
    cols = forward(swap(cols, "tile"))
    rows = call(column_kernel, shape((groups, 16, LANES), F32), [cols, weight, kt])
    rows, opposite = lax.optimization_barrier((rows, opposite))
    rows = swap(rows, "grp")
    every = before + [opposite] + after[:0:-1]
    cols, later = call(wide_row_kernel, (wide, tile), [rows, mass] + every)
    for _ in range(SCALING_ROUNDS - 3):
        cols = swap(cols, "tile")
        cols = call(wide_round_kernel, wide, [cols, later, weights] + every)
    cols = swap(cols, "tile")
    scaled = call(
        last_round_kernel, shape((tiles, 40, LANES), F32), [cols, later, weights] + every
    )
    scaled = swap(scaled, "tile")
    return call(
        functools.partial(plan_kernel, float(cells * tiles)),
        shape((1, cells, LANES), F32),
        [scaled, weight],
        scratch=[pltpu.VMEM((1, cells, LANES), F32), pltpu.SemaphoreType.DMA((tiles // 8,))],
        out_hbm=True,
    )


def solution(mesh):
    return jax.shard_map(
        body,
        mesh=mesh,
        in_specs=(
            P("tile", "grp"),
            P("tile"),
            P("tile", None),
            P("tile"),
            P("tile", None),
            P("tile", None),
            P("grp"),
            P("grp"),
        ),
        out_specs=P("tile", None, "grp"),
        check_vma=False,
    )
```

time: 675 us -> 162 us (0.24)
  blocking collectives: 390 us -> 105 us
  waiting for transfers between devices: 95.3 us -> 16.8 us
  other arithmetic: 79 us -> 0.66 us
  starting transfers between devices: 66.9 us -> 19.8 us
  local copies, waits for them, and re-layouts: 36.5 us -> 0.62 us
  Pallas kernels: 0 us -> 17.9 us
    psum x10 -> x0, blocking collectives: 390 us -> none  [the longest x5 328 us: scale_plan(): col_sums = lax.psum(partial_cols, 'tile')]
    all_to_all x0 -> x8, blocking collectives: none -> 105 us  [swap(): return lax.all_to_all(values, axis, split_axis=0, concat_axis=0, tiled=True)]
    ppermute x20 -> x7, waiting for transfers between devices: 95.3 us -> 0.02 us  [the longest x2 0.01 us: forward(): before.append(lax.ppermute(last, 'grp', up))]
    scatter-add x2 -> x0, other arithmetic: 56 us -> none  [the longest x1 28.8 us: body(): cell_mass = jnp.zeros((cells_local,), jnp.float32).at[flat_cell].add(got_...]
    ppermute x20 -> x7, starting transfers between devices: 43.6 us -> 11.1 us  [the longest x1 5.66 us: body(): after = [kt, lax.ppermute(short, 'grp', down)]]
    scatter x3 -> x0, local copies, waits for them, and re-layouts: 30.7 us -> none  [the longest x1 14.8 us: body(): jnp.zeros((slot_total,), jnp.bfloat16).at[target_slot].set(spot_weight)]
    pallas_call x0 -> x12, Pallas kernels: none -> 17.9 us  [call(): pl.pallas_call(kernel, out_shape=out_shape, in_specs=specs, out_specs=out...]
    all_to_all x3 -> x1, waiting for transfers between devices: 0.01 us -> 16.7 us  [swap(): return lax.all_to_all(values, axis, split_axis=0, concat_axis=0, tiled=True)]
  transfers between devices with their start and end apart: 23 -> 8, of which waited for: 20 -> 1; matrix products, arithmetic and copies ran while one was open for 7% -> 1% of each run, Pallas kernels for 0% -> 0%
where the time goes in v1:
time: 162 us; the launch traced here: 161 us
  blocking collectives  105 us (65%)
  starting transfers between devices  19.8 us (12%)
  Pallas kernels  17.9 us (11%)
  waiting for transfers between devices  16.8 us (10%)
    all_to_all x8, blocking collectives, swap(): return lax.all_to_all(values, axis, split_axis=0, concat_axis=0, tiled=True)  105 us
    pallas_call x12, Pallas kernels, call(): pl.pallas_call(kernel, out_shape=out_shape, in_specs=specs, out_specs=out...  17.9 us
    all_to_all x1, waiting for transfers between devices, swap(): return lax.all_to_all(values, axis, split_axis=0, concat_axis=0, tiled=True)  16.7 us
    all_to_all x1, starting transfers between devices, swap(): return lax.all_to_all(values, axis, split_axis=0, concat_axis=0, tiled=True)  8.73 us
    ppermute x1, starting transfers between devices, body(): after = [kt, lax.ppermute(short, 'grp', down)]  5.66 us
    ppermute x2, starting transfers between devices, forward(): after.append(lax.ppermute(first, 'grp', down))  4.71 us
  transfers between devices with their start and end apart: 8, of which 1 were waited for; matrix products, arithmetic and copies ran while one was open for 1% of the time, Pallas kernels for 0%

profile of v1, /device:TPU:1, one launch (start us, length us, event | category | flops | bytes accessed | tf_op | source)
XLA Modules:
  0.0 161.1 jit_solution(7999008403996228047)
XLA Ops:
  0.0 6.8 %shard_map.82 = bf16[32,144,128]{2,1,0:T(8,128)(2,1)} custom-call(s32[1,2048]{1,0:T(1,128)} %bitcast.9, s32[1,2048]{1,0:T(1,128)} %bitcast.10, bf16[16,128]{1,0:T(8,128)(2,1)} %bitcast.11, bf16[2048,128]{1,0:T(8,128)(2,1)} %terms_hbm.1), custom_call_target="tpu_custom_call" | custom-call | tf_op jit(solution)/shard_map/pallas_call | solution.py:34
  6.8 0.0 copy-start.3
  6.8 0.0 copy-start.1
  6.8 8.7 %all-to-all-start = ((bf16[32,144,128]{2,1,0:T(8,128)(2,1)}), bf16[32,144,128]{2,1,0:T(8,128)(2,1)S(1)}, u32[]{:S(2)}, u32[]{:S(2)}) async-start(bf16[32,144,128]{2,1,0:T(8,128)(2,1)} %shard_map.82), calls=%async_computation | async-start | bytes 2359296 | tf_op jit(solution)/shard_map/all_to_all | solution.py:379
  15.6 0.5 broadcast.5
  16.1 0.7 reduce.3
  16.8 0.1 reshape.22
  16.8 0.3 shard_map.83
  17.2 16.7 %all-to-all-done.msg_ref = bf16[32,144,128]{2,1,0:T(8,128)(2,1)S(1)} async-done(((bf16[32,144,128]{2,1,0:T(8,128)(2,1)}), bf16[32,144,128]{2,1,0:T(8,128)(2,1)S(1)}, u32[]{:S(2)}, u32[]{:S(2)}) %all-to-all-start) | async-done | bytes 1179680 | tf_op jit(solution)/shard_map/all_to_all | solution.py:379
  33.9 3.8 %shard_map.84 = f32[32,40,128]{2,1,0:T(8,128)S(1)} custom-call(bf16[32,144,128]{2,1,0:T(8,128)(2,1)S(1)} %all-to-all-done.msg_ref, f32[1024,128]{1,0:T(8,128)S(1)} %get-tuple-element.23.ccol_ref, f32[32,128]{1,0:T(8,128)S(1)} %pad.4.rcoef_ref), custom_call_target="tpu_custom_call" | custom-call | tf_op jit(solution)/shard_map/pallas_call | solution.py:34
  37.7 16.7 %all_to_all.45.msg_ref = f32[32,40,128]{2,1,0:T(8,128)S(1)} all-to-all(f32[32,40,128]{2,1,0:T(8,128)S(1)} %shard_map.84), channel_id=1, replica_groups=mesh['grp'=8,'tile'=32] {'tile'}, dimensions={0} | all-to-all | bytes 1310720 | tf_op jit(solution)/shard_map/all_to_all | solution.py:379
  54.4 2.1 %shard_map.85 = (f32[128,1024]{1,0:T(8,128)S(1)}, bf16[128,1024]{1,0:T(8,128)(2,1)S(1)}, f32[8,128]{1,0:T(8,128)S(1)}, f32[8,16,128]{2,1,0:T(8,128)S(1)}) custom-call(f32[32,40,128]{2,1,0:T(8,128)S(1)} %all_to_all.45.msg_ref, f32[128,128]{1,0:T(8,128)S(1)} %get-tuple-element.24.patch_ref, f32[1,128]{1,0:T(1,128)S(1)} %bitcast.5), custom_call_target="tpu_custom_call" | custom-call | tf_op jit(solution)/shard_map/pallas_call | solution.py:34
  56.5 5.7 %collective-permute-start.1 = (bf16[128,1024]{1,0:T(8,128)(2,1)S(1)}, bf16[128,1024]{1,0:T(8,128)(2,1)S(1)}, u32[]{:S(2)}, u32[]{:S(2)}) collective-permute-start(bf16[128,1024]{1,0:T(8,128)(2,1)S(1)} %get-tuple-element.26), channel_id=1, source_target_pairs={{0,224},{32,0},{64,32},{96,64},{128,96},{160,128},{192,160},{224,1... | collective-permute-start | bytes 786440 | tf_op jit(solution)/shard_map/ppermute | solution.py:442
  62.2 11.1 %all_to_all.46.msg_ref = f32[8,16,128]{2,1,0:T(8,128)S(1)} all-to-all(f32[8,16,128]{2,1,0:T(8,128)S(1)} %get-tuple-element.25), channel_id=1, replica_groups=mesh['grp'=8,'tile'=32] {'grp'}, dimensions={0} | all-to-all | bytes 131072 | tf_op jit(solution)/shard_map/all_to_all | solution.py:379
  73.3 0.3 collective-permute-start.2
  73.6 2.4 %collective-permute-start.3 = (bf16[128,1024]{1,0:T(8,128)(2,1)S(1)}, bf16[128,1024]{1,0:T(8,128)(2,1)S(1)}, u32[]{:S(2)}, u32[]{:S(2)}) collective-permute-start(bf16[128,1024]{1,0:T(8,128)(2,1)S(1)} %collective-permute-done.1.even_ref.refs_7_), channel_id=1, source_target_pairs={{0,224},{32,0},{64,32},{96,64},{128,96},{160,128},{192,160},{224,1... | collective-permute-start | bytes 786440 | tf_op jit(solution)/shard_map/ppermute | solution.py:449
  76.0 0.1 collective-permute-start.4
  76.1 0.1 shard_map.86
  76.2 13.0 %all_to_all.47.msg_ref = f32[32,1,128]{2,1,0:T(1,128)S(1)} all-to-all(f32[32,1,128]{2,1,0:T(1,128)S(1)} %get-tuple-element.30), channel_id=1, replica_groups=mesh['grp'=8,'tile'=32] {'tile'}, dimensions={0} | all-to-all | bytes 32768 | tf_op jit(solution)/shard_map/all_to_all | solution.py:379
  89.2 0.4 collective-permute-start.5
  89.6 2.3 %collective-permute-start.6 = (bf16[128,1024]{1,0:T(8,128)(2,1)S(1)}, bf16[128,1024]{1,0:T(8,128)(2,1)S(1)}, u32[]{:S(2)}, u32[]{:S(2)}) collective-permute-start(bf16[128,1024]{1,0:T(8,128)(2,1)S(1)} %collective-permute-done.3.refs_6_), channel_id=1, source_target_pairs={{0,224},{32,0},{64,32},{96,64},{128,96},{160,128},{192,160},{224,1... | collective-permute-start | bytes 786440 | tf_op jit(solution)/shard_map/ppermute | solution.py:449
  91.9 0.1 shard_map.87
  92.0 11.8 %all_to_all.48.msg_ref = f32[8,16,128]{2,1,0:T(8,128)S(1)} all-to-all(f32[8,16,128]{2,1,0:T(8,128)S(1)} %shard_map.87), channel_id=1, replica_groups=mesh['grp'=8,'tile'=32] {'grp'}, dimensions={0} | all-to-all | bytes 131072 | tf_op jit(solution)/shard_map/all_to_all | solution.py:379
  103.9 0.9 shard_map.89
  104.8 13.4 %all_to_all.49.msg_ref = f32[32,8,128]{2,1,0:T(8,128)S(1)} all-to-all(f32[32,8,128]{2,1,0:T(8,128)S(1)} %get-tuple-element.38), channel_id=1, replica_groups=mesh['grp'=8,'tile'=32] {'tile'}, dimensions={0} | all-to-all | bytes 262144 | tf_op jit(solution)/shard_map/all_to_all | solution.py:379
  118.2 1.0 shard_map.90
  119.2 11.3 %all_to_all.50.msg_ref = f32[32,8,128]{2,1,0:T(8,128)S(1)} all-to-all(f32[32,8,128]{2,1,0:T(8,128)S(1)} %shard_map.90), channel_id=1, replica_groups=mesh['grp'=8,'tile'=32] {'tile'}, dimensions={0} | all-to-all | bytes 262144 | tf_op jit(solution)/shard_map/all_to_all | solution.py:379
  130.5 1.0 shard_map.91
  131.5 11.3 %all_to_all.51.msg_ref = f32[32,8,128]{2,1,0:T(8,128)S(1)} all-to-all(f32[32,8,128]{2,1,0:T(8,128)S(1)} %shard_map.91), channel_id=1, replica_groups=mesh['grp'=8,'tile'=32] {'tile'}, dimensions={0} | all-to-all | bytes 262144 | tf_op jit(solution)/shard_map/all_to_all | solution.py:379
  142.8 0.8 shard_map.92
  143.6 16.5 %all_to_all.52.msg_ref = f32[32,40,128]{2,1,0:T(8,128)S(1)} all-to-all(f32[32,40,128]{2,1,0:T(8,128)S(1)} %shard_map.92), channel_id=1, replica_groups=mesh['grp'=8,'tile'=32] {'tile'}, dimensions={0} | all-to-all | bytes 1310720 | tf_op jit(solution)/shard_map/all_to_all | solution.py:379
  160.1 0.8 shard_map.93
  (16 shorter events, 0.1 us)
Async XLA Ops:
  6.8 9.3 %copy-start.3 = (f32[1,1024]{1,0:T(1,128)S(1)}, f32[1,1024]{1,0:T(1,128)}, u32[]{:S(2)}) copy-start(f32[1,1024]{1,0:T(1,128)} %param.13) | copy-start | bytes 12292
  6.8 10.0 %copy-start.1 = (f32[1,1024]{1,0:T(1,128)S(1)}, f32[1,1024]{1,0:T(1,128)}, u32[]{:S(2)}) copy-start(f32[1,1024]{1,0:T(1,128)} %col_ref.1) | copy-start | bytes 12292
  6.8 10.0 %copy-start.2 = (f32[128]{0:T(128)S(1)}, f32[128]{0:T(128)}, u32[]{:S(2)}) copy-start(f32[128]{0:T(128)} %param.14) | copy-start | bytes 1540
  6.8 27.1 %all-to-all-start = ((bf16[32,144,128]{2,1,0:T(8,128)(2,1)}), bf16[32,144,128]{2,1,0:T(8,128)(2,1)S(1)}, u32[]{:S(2)}, u32[]{:S(2)}) async-start(bf16[32,144,128]{2,1,0:T(8,128)(2,1)} %shard_map.82), calls=%async_computation | async-start | bytes 2359296 | tf_op jit(solution)/shard_map/all_to_all | solution.py:379
  37.7 16.7 %copy-start = (f32[128]{0:T(128)S(1)}, f32[128]{0:T(128)}, u32[]{:S(2)}) copy-start(f32[128]{0:T(128)} %param.15) | copy-start | bytes 1540
  56.5 16.8 %collective-permute-start.1 = (bf16[128,1024]{1,0:T(8,128)(2,1)S(1)}, bf16[128,1024]{1,0:T(8,128)(2,1)S(1)}, u32[]{:S(2)}, u32[]{:S(2)}) collective-permute-start(bf16[128,1024]{1,0:T(8,128)(2,1)S(1)} %get-tuple-element.26), channel_id=1, source_target_pairs={{0,224},{32,0},{64,32},{96,64},{128,96},{160,128},{192,160},{224,1... | collective-permute-start | bytes 786440 | tf_op jit(solution)/shard_map/ppermute | solution.py:442
  62.2 11.1 %collective-permute-start = (bf16[128,1024]{1,0:T(8,128)(2,1)S(1)}, bf16[128,1024]{1,0:T(8,128)(2,1)S(1)}, u32[]{:S(2)}, u32[]{:S(2)}) collective-permute-start(bf16[128,1024]{1,0:T(8,128)(2,1)S(1)} %get-tuple-element.26), channel_id=1, source_target_pairs={{0,32},{32,64},{64,96},{96,128},{128,160},{160,192},{192,224},{224... | collective-permute-start | bytes 786440 | tf_op jit(solution)/shard_map/ppermute | solution.py:441
  73.3 15.9 %collective-permute-start.2 = (bf16[128,1024]{1,0:T(8,128)(2,1)S(1)}, bf16[128,1024]{1,0:T(8,128)(2,1)S(1)}, u32[]{:S(2)}, u32[]{:S(2)}) collective-permute-start(bf16[128,1024]{1,0:T(8,128)(2,1)S(1)} %collective-permute-done.odd_ref.refs_1_), channel_id=1, source_target_pairs={{0,32},{32,64},{64,96},{96,128},{128,160},{160,192},{192,224},{224... | collective-permute-start | bytes 786440 | tf_op jit(solution)/shard_map/ppermute | solution.py:448
  73.6 15.6 %collective-permute-start.3 = (bf16[128,1024]{1,0:T(8,128)(2,1)S(1)}, bf16[128,1024]{1,0:T(8,128)(2,1)S(1)}, u32[]{:S(2)}, u32[]{:S(2)}) collective-permute-start(bf16[128,1024]{1,0:T(8,128)(2,1)S(1)} %collective-permute-done.1.even_ref.refs_7_), channel_id=1, source_target_pairs={{0,224},{32,0},{64,32},{96,64},{128,96},{160,128},{192,160},{224,1... | collective-permute-start | bytes 786440 | tf_op jit(solution)/shard_map/ppermute | solution.py:449
  76.0 16.0 %collective-permute-start.4 = (bf16[128,1024]{1,0:T(8,128)(2,1)S(1)}, bf16[128,1024]{1,0:T(8,128)(2,1)S(1)}, u32[]{:S(2)}, u32[]{:S(2)}) collective-permute-start(bf16[128,1024]{1,0:T(8,128)(2,1)S(1)} %shard_map.88), channel_id=1, source_target_pairs={{0,160},{1,97},{2,162},{3,99},{4,164},{5,101},{6,166},{7,103},{8,1... | collective-permute-start | bytes 786440 | tf_op jit(solution)/shard_map/ppermute | solution.py:459
  89.2 14.7 %collective-permute-start.5 = (bf16[128,1024]{1,0:T(8,128)(2,1)S(1)}, bf16[128,1024]{1,0:T(8,128)(2,1)S(1)}, u32[]{:S(2)}, u32[]{:S(2)}) collective-permute-start(bf16[128,1024]{1,0:T(8,128)(2,1)S(1)} %collective-permute-done.2.refs_2_), channel_id=1, source_target_pairs={{0,32},{32,64},{64,96},{96,128},{128,160},{160,192},{192,224},{224... | collective-permute-start | bytes 786440 | tf_op jit(solution)/shard_map/ppermute | solution.py:448
  89.6 14.3 %collective-permute-start.6 = (bf16[128,1024]{1,0:T(8,128)(2,1)S(1)}, bf16[128,1024]{1,0:T(8,128)(2,1)S(1)}, u32[]{:S(2)}, u32[]{:S(2)}) collective-permute-start(bf16[128,1024]{1,0:T(8,128)(2,1)S(1)} %collective-permute-done.3.refs_6_), channel_id=1, source_target_pairs={{0,224},{32,0},{64,32},{96,64},{128,96},{160,128},{192,160},{224,1... | collective-permute-start | bytes 786440 | tf_op jit(solution)/shard_map/ppermute | solution.py:449

commit v2 on v1

--- a/solution.py
+++ b/solution.py
@@ -14,6 +14,7 @@
 LANES = 128
 CAP = 128
 META = 16
+PART = 33
 F32 = jnp.float32
 BF16 = jnp.bfloat16
 NT = (((1,), (1,)), ((), ()))
@@ -94,8 +95,8 @@
     kind = which % 8
     value = jnp.where(kind == 0, weight, jnp.where(kind == 1, high, jnp.where(kind == 2, low, 0.0)))
     value = jnp.where(which // 8 == owner, value, 0.0).astype(BF16)
-    onehot_ref[1, 0:CAP, :] = onehot_rows(rank, 0, CAP)
-    meta = lax.dot_general(value, onehot_ref[1, 0:CAP, :], NT, preferred_element_type=F32)
+    onehot_ref[0:CAP, :] = onehot_rows(rank, 0, CAP)
+    meta = lax.dot_general(value, onehot_ref[0:CAP, :], NT, preferred_element_type=F32)
     empty = jnp.zeros((8, LANES), F32)
     for t in range(tiles):
         out_ref[t, CAP : CAP + META, :] = jnp.concatenate(
@@ -104,8 +105,8 @@
     terms = terms_ref[...]
     leaving = []
     for chunk in range(tiles * CAP // 256):
-        onehot_ref[chunk % 2] = onehot_rows(slot, chunk * 256, 256)
-        rows = jnp.dot(onehot_ref[chunk % 2], terms, preferred_element_type=F32).astype(BF16)
+        onehot_ref[...] = onehot_rows(slot, chunk * 256, 256)
+        rows = jnp.dot(onehot_ref[...], terms, preferred_element_type=F32).astype(BF16)
         out_ref[2 * chunk, 0:CAP, :] = rows[:CAP]
         out_ref[2 * chunk + 1, 0:CAP, :] = rows[CAP:]
         both = pl.ds(2 * chunk, 2)
@@ -156,9 +157,9 @@
         ref[0:8, :] = pad
         ref[8 + cells : 16 + cells, :] = pad
     for chunk in range(cells // 256):
-        onehot_ref[chunk % 2] = onehot_rows(cell, chunk * 256, 256)
+        onehot_ref[...] = onehot_rows(cell, chunk * 256, 256)
         a_ref[8 + 256 * chunk : 8 + 256 * (chunk + 1), :] = jnp.dot(
-            onehot_ref[chunk % 2], rows, preferred_element_type=F32
+            onehot_ref[...], rows, preferred_element_type=F32
         )
     blocks = cells // PATCH_ROW
     lane_shift = (lax.rem(lax.axis_index("tile"), 4) * 32).astype(F32)
@@ -166,31 +167,26 @@
     lower = (iota((LANES, slots), 0).astype(F32) == low + lane_shift).astype(F32).astype(BF16)
     mass = lax.dot_general(upper, lower, NT, preferred_element_type=F32)
 
-    def heated(src, c, size):
-        o = 8 + c * size
-        mid = src[o : o + size, :]
-        beside = src[o - 1 : o - 1 + size, :] + src[o + 1 : o + 1 + size, :]
-        coef = ccol_ref[c * size : (c + 1) * size, :]
-        return mid + coef * (beside - 2.0 * mid)
-
     def step(src, dst):
         size = 128
         for c in range(cells // size):
-            dst[8 + c * size : 8 + (c + 1) * size, :] = heated(src, c, size)
+            o = 8 + c * size
+            mid = src[o : o + size, :]
+            beside = src[o - 1 : o - 1 + size, :] + src[o + 1 : o + 1 + size, :]
+            coef = ccol_ref[c * size : (c + 1) * size, :]
+            dst[o : o + size, :] = mid + coef * (beside - 2.0 * mid)
 
     def two_steps(_, carry):
         step(a_ref, b_ref)
         step(b_ref, a_ref)
         return carry
 
-    lax.fori_loop(0, HEAT_STEPS // 2 - 1, two_steps, 0)
-    step(a_ref, b_ref)
-    sub = iota((8, LANES), 0)
+    lax.fori_loop(0, HEAT_STEPS // 2, two_steps, 0)
+    shift = lax.rem(lax.axis_index("tile") + 2, 4) * 32
+    extra = mass + pltpu.roll(rcoef_ref[...], shift, 1)
     for d in range(tiles):
-        out_ref[d, 0:32, :] = heated(b_ref, d, 32)
-        out_ref[d, 32:40, :] = jnp.where(
-            sub == 0, rcoef_ref[d : d + 1, :], jnp.where(sub == 1, mass[d : d + 1, :], 0.0)
-        )
+        out_ref[PART * d : PART * d + 32, :] = a_ref[8 + 32 * d : 40 + 32 * d, :]
+        out_ref[PART * d + 32 : PART * d + 33, :] = extra[d : d + 1, :]
 
 
 def tile_of(parts):
@@ -214,19 +210,21 @@
 def band_kernel(
     msg_ref, patch_ref, weight_ref, kt_ref, short_ref, mass_ref, out_ref, coef_ref, field_ref
 ):
-    tiles = msg_ref.shape[0]
-    sub = iota((8, LANES), 0)
+    tiles = msg_ref.shape[0] // PART
+    owner = iota((8, LANES), 0) * 4 + iota((8, LANES), 1) // 32
+    extra = [msg_ref[PART * r + 32 : PART * r + 33, :] for r in range(tiles)]
     mass = jnp.zeros((8, LANES), F32)
     coef = []
     for r in range(tiles):
-        mass = mass + jnp.where(sub == r // 4, msg_ref[r, 33:34, :], 0.0)
+        mass = jnp.where(owner == r, extra[r], mass)
     mass_ref[...] = mass
     for b in range(tiles // 8):
-        coef.append(tile_of([msg_ref[8 * b + r, 32:33, :] for r in range(8)]))
+        coef.append(tile_of(extra[8 * b : 8 * b + 8]))
     coef.append(jnp.zeros((LANES - tiles, LANES), F32))
     coef = jnp.concatenate(coef, axis=0).T
     for r in range(tiles):
-        coef_ref[r, :, :] = jnp.broadcast_to(coef[0:32, r : r + 1], (32, LANES))
+        at = 32 * ((r + 2) % 4)
+        coef_ref[r, :, :] = jnp.broadcast_to(coef[at : at + 32, r : r + 1], (32, LANES))
     zero = jnp.zeros((8, LANES), F32)
     for b in range(4):
         place = slice(8 * b, 8 * b + 8)
@@ -240,7 +238,7 @@
             return tuple(out)
 
         field = lax.fori_loop(
-            0, HEAT_STEPS, step, tuple(msg_ref[r, place, :] for r in range(tiles))
+            0, HEAT_STEPS, step, tuple(msg_ref[PART * r + 8 * b : PART * r + 8 * b + 8, :] for r in range(tiles))
         )
         for r in range(tiles):
             field_ref[32 * r + 8 * b : 32 * r + 8 * b + 8, :] = field[r]
@@ -351,32 +349,27 @@
         turned = pieces[t].T
         column = column + jnp.sum(turned, axis=0, keepdims=True)
         for r in range(4):
-            out_ref[4 * t + r, 0:32, :] = turned[32 * r : 32 * r + 32]
-    for r in range(out_ref.shape[0]):
-        out_ref[r, 32:40, :] = jnp.broadcast_to(column, (8, LANES))
-
-
-def plan_kernel(cell_count, msg_ref, weight_ref, out_hbm, plan_ref, sems):
-    tiles = msg_ref.shape[0]
-    scale = column_scale([msg_ref[t, 32:33, :] for t in range(tiles)], weight_ref[...])
-    scale = scale * cell_count
-    copies = []
+            at = PART * (4 * t + r)
+            out_ref[at : at + 32, :] = turned[32 * r : 32 * r + 32]
+    for at in range(32, out_ref.shape[0], PART):
+        out_ref[at : at + 1, :] = column
+
+
+def plan_kernel(cell_count, msg_ref, weight_ref, out_ref):
+    tiles = msg_ref.shape[0] // PART
+    sums = [msg_ref[PART * t + 32 : PART * t + 33, :] for t in range(tiles)]
+    scale = column_scale(sums, weight_ref[...]) * cell_count
     for d in range(tiles):
-        plan_ref[0, 32 * d : 32 * d + 32, :] = msg_ref[d, 0:32, :] * scale
-        if d % 8 == 7:
-            rows = pl.ds(32 * (d - 7), 256)
-            copies.append(
-                pltpu.make_async_copy(
-                    plan_ref.at[:, rows], out_hbm.at[:, rows], sems.at[d // 8]
-                )
-            )
-            copies[-1].start()
-    for copy in copies:
-        copy.wait()
+        out_ref[0, 32 * d : 32 * d + 32, :] = msg_ref[PART * d : PART * d + 32, :] * scale
 
 
 def swap(values, axis):
     return lax.all_to_all(values, axis, split_axis=0, concat_axis=0, tiled=True)
+
+
+def swap_parts(parts, axis):
+    size = lax.axis_size(axis)
+    return swap(parts.reshape(size, PART, 1, LANES), axis).reshape(size * PART, LANES)
 
 
 def body(spot_terms, spot_weight, spot_owner, spot_cell, col_coef, row_coef, tgt_coef, tgt_weight):
@@ -398,7 +391,7 @@
         ],
         scratch=[
             pltpu.VMEM((tiles, CAP + META, columns), BF16),
-            pltpu.VMEM((2, 256, spots), BF16),
+            pltpu.VMEM((256, spots), BF16),
             pltpu.VMEM((1, spots), jnp.int32),
             pltpu.VMEM((1, spots), jnp.int32),
             pltpu.VMEM((spots // LANES, LANES), BF16),
@@ -418,15 +411,15 @@
     got = swap(packed, "tile")
     sorted_field = call(
         gather_kernel,
-        shape((tiles, 40, LANES), F32),
+        shape((tiles * PART, LANES), F32),
         [got, ccol, rcoef],
         scratch=[
-            pltpu.VMEM((2, 256, tiles * CAP), BF16),
+            pltpu.VMEM((256, tiles * CAP), BF16),
             pltpu.VMEM((cells + 16, LANES), F32),
             pltpu.VMEM((cells + 16, LANES), F32),
         ],
     )
-    band = swap(sorted_field, "tile")
+    band = swap_parts(sorted_field, "tile")
     tile = shape((8, LANES), F32)
     wide = shape((tiles, groups, LANES), F32)
     field = (columns, cells)
@@ -469,15 +462,13 @@
         cols = call(wide_round_kernel, wide, [cols, later, weights] + every)
     cols = swap(cols, "tile")
     scaled = call(
-        last_round_kernel, shape((tiles, 40, LANES), F32), [cols, later, weights] + every
-    )
-    scaled = swap(scaled, "tile")
+        last_round_kernel, shape((tiles * PART, LANES), F32), [cols, later, weights] + every
+    )
+    scaled = swap_parts(scaled, "tile")
     return call(
         functools.partial(plan_kernel, float(cells * tiles)),
         shape((1, cells, LANES), F32),
         [scaled, weight],
-        scratch=[pltpu.VMEM((1, cells, LANES), F32), pltpu.SemaphoreType.DMA((tiles // 8,))],
-        out_hbm=True,
     )
 
 

time: 162 us -> 160 us (0.988)
  blocking collectives: 105 us -> 103 us
    all_to_all x8, blocking collectives: 105 us -> 103 us  [swap(): return lax.all_to_all(values, axis, split_axis=0, concat_axis=0, tiled=True)]
where the time goes in v2:
time: 160 us; the launch traced here: 159 us
  blocking collectives  103 us (64%)
  starting transfers between devices  19.8 us (12%)
  Pallas kernels  18.4 us (11%)
  waiting for transfers between devices  16.8 us (10%)
    all_to_all x8, blocking collectives, swap(): return lax.all_to_all(values, axis, split_axis=0, concat_axis=0, tiled=True)  103 us
    pallas_call x12, Pallas kernels, call(): pl.pallas_call(kernel, out_shape=out_shape, in_specs=specs, out_specs=out...  18.4 us
    all_to_all x1, waiting for transfers between devices, swap(): return lax.all_to_all(values, axis, split_axis=0, concat_axis=0, tiled=True)  16.7 us
    all_to_all x1, starting transfers between devices, swap(): return lax.all_to_all(values, axis, split_axis=0, concat_axis=0, tiled=True)  8.73 us
    ppermute x1, starting transfers between devices, body(): after = [kt, lax.ppermute(short, 'grp', down)]  5.65 us
    ppermute x2, starting transfers between devices, forward(): after.append(lax.ppermute(first, 'grp', down))  4.71 us
  transfers between devices with their start and end apart: 8, of which 1 were waited for; matrix products, arithmetic and copies ran while one was open for 1% of the time, Pallas kernels for 0%

profile of v2, /device:TPU:1, one launch (start us, length us, event | category | flops | bytes accessed | tf_op | source)
XLA Modules:
  0.0 159.1 jit_solution(17706283451929296904)
XLA Ops:
  0.0 6.8 %shard_map.82 = bf16[32,144,128]{2,1,0:T(8,128)(2,1)} custom-call(s32[1,2048]{1,0:T(1,128)} %bitcast.17, s32[1,2048]{1,0:T(1,128)} %bitcast.18, bf16[16,128]{1,0:T(8,128)(2,1)} %bitcast.19, bf16[2048,128]{1,0:T(8,128)(2,1)} %terms_hbm.1), custom_call_target="tpu_custom_call" | custom-call | tf_op jit(solution)/shard_map/pallas_call | solution.py:35
  6.8 0.0 copy-start.3
  6.8 0.0 copy-start.2
  6.8 8.7 %all-to-all-start = ((bf16[32,144,128]{2,1,0:T(8,128)(2,1)}), bf16[32,144,128]{2,1,0:T(8,128)(2,1)S(1)}, u32[]{:S(2)}, u32[]{:S(2)}) async-start(bf16[32,144,128]{2,1,0:T(8,128)(2,1)} %shard_map.82), calls=%async_computation | async-start | bytes 2359296 | tf_op jit(solution)/shard_map/all_to_all | solution.py:367
  15.6 0.5 broadcast.5
  16.1 0.7 reduce.3
  16.8 0.1 reshape.34
  16.8 0.3 shard_map.83
  17.2 16.7 %all-to-all-done.msg_ref = bf16[32,144,128]{2,1,0:T(8,128)(2,1)S(1)} async-done(((bf16[32,144,128]{2,1,0:T(8,128)(2,1)}), bf16[32,144,128]{2,1,0:T(8,128)(2,1)S(1)}, u32[]{:S(2)}, u32[]{:S(2)}) %all-to-all-start) | async-done | bytes 1179680 | tf_op jit(solution)/shard_map/all_to_all | solution.py:367
  33.9 4.4 %shard_map.84 = f32[1056,128]{1,0:T(8,128)S(1)} custom-call(bf16[32,144,128]{2,1,0:T(8,128)(2,1)S(1)} %all-to-all-done.msg_ref, f32[1024,128]{1,0:T(8,128)S(1)} %get-tuple-element.23.ccol_ref, f32[32,128]{1,0:T(8,128)S(1)} %pad.4.rcoef_ref), custom_call_target="tpu_custom_call" | custom-call | tf_op jit(solution)/shard_map/pallas_call | solution.py:35
  38.3 15.5 %all_to_all.45 = f32[32,33,1,128]{3,2,1,0:T(1,128)S(1)} all-to-all(f32[32,33,1,128]{3,2,1,0:T(1,128)S(1)} %bitcast.11), channel_id=1, replica_groups=mesh['grp'=8,'tile'=32] {'tile'}, dimensions={0} | all-to-all | bytes 1081344 | tf_op jit(solution)/shard_map/all_to_all | solution.py:367
  53.8 2.1 %shard_map.85 = (f32[128,1024]{1,0:T(8,128)S(1)}, bf16[128,1024]{1,0:T(8,128)(2,1)S(1)}, f32[8,128]{1,0:T(8,128)S(1)}, f32[8,16,128]{2,1,0:T(8,128)S(1)}) custom-call(f32[1056,128]{1,0:T(8,128)S(1)} %bitcast.10, f32[128,128]{1,0:T(8,128)S(1)} %get-tuple-element.24.patch_ref, f32[1,128]{1,0:T(1,128)S(1)} %bitcast.13), custom_call_target="tpu_custom_call" | custom-call | tf_op jit(solution)/shard_map/pallas_call | solution.py:35
  55.9 5.7 %collective-permute-start.1 = (bf16[128,1024]{1,0:T(8,128)(2,1)S(1)}, bf16[128,1024]{1,0:T(8,128)(2,1)S(1)}, u32[]{:S(2)}, u32[]{:S(2)}) collective-permute-start(bf16[128,1024]{1,0:T(8,128)(2,1)S(1)} %get-tuple-element.26), channel_id=1, source_target_pairs={{0,224},{32,0},{64,32},{96,64},{128,96},{160,128},{192,160},{224,1... | collective-permute-start | bytes 786440 | tf_op jit(solution)/shard_map/ppermute | solution.py:435
  61.6 11.1 %all_to_all.46.msg_ref = f32[8,16,128]{2,1,0:T(8,128)S(1)} all-to-all(f32[8,16,128]{2,1,0:T(8,128)S(1)} %get-tuple-element.25), channel_id=1, replica_groups=mesh['grp'=8,'tile'=32] {'grp'}, dimensions={0} | all-to-all | bytes 131072 | tf_op jit(solution)/shard_map/all_to_all | solution.py:367
  72.7 0.3 collective-permute-start.2
  73.0 2.4 %collective-permute-start.3 = (bf16[128,1024]{1,0:T(8,128)(2,1)S(1)}, bf16[128,1024]{1,0:T(8,128)(2,1)S(1)}, u32[]{:S(2)}, u32[]{:S(2)}) collective-permute-start(bf16[128,1024]{1,0:T(8,128)(2,1)S(1)} %collective-permute-done.1.even_ref.refs_7_), channel_id=1, source_target_pairs={{0,224},{32,0},{64,32},{96,64},{128,96},{160,128},{192,160},{224,1... | collective-permute-start | bytes 786440 | tf_op jit(solution)/shard_map/ppermute | solution.py:442
  75.4 0.1 collective-permute-start.4
  75.5 0.1 shard_map.86
  75.6 12.9 %all_to_all.47.msg_ref = f32[32,1,128]{2,1,0:T(1,128)S(1)} all-to-all(f32[32,1,128]{2,1,0:T(1,128)S(1)} %get-tuple-element.30), channel_id=1, replica_groups=mesh['grp'=8,'tile'=32] {'tile'}, dimensions={0} | all-to-all | bytes 32768 | tf_op jit(solution)/shard_map/all_to_all | solution.py:367
  88.6 0.4 collective-permute-start.5
  88.9 2.3 %collective-permute-start.6 = (bf16[128,1024]{1,0:T(8,128)(2,1)S(1)}, bf16[128,1024]{1,0:T(8,128)(2,1)S(1)}, u32[]{:S(2)}, u32[]{:S(2)}) collective-permute-start(bf16[128,1024]{1,0:T(8,128)(2,1)S(1)} %collective-permute-done.3.refs_6_), channel_id=1, source_target_pairs={{0,224},{32,0},{64,32},{96,64},{128,96},{160,128},{192,160},{224,1... | collective-permute-start | bytes 786440 | tf_op jit(solution)/shard_map/ppermute | solution.py:442
  91.2 0.1 shard_map.87
  91.4 11.8 %all_to_all.48.msg_ref = f32[8,16,128]{2,1,0:T(8,128)S(1)} all-to-all(f32[8,16,128]{2,1,0:T(8,128)S(1)} %shard_map.87), channel_id=1, replica_groups=mesh['grp'=8,'tile'=32] {'grp'}, dimensions={0} | all-to-all | bytes 131072 | tf_op jit(solution)/shard_map/all_to_all | solution.py:367
  103.2 0.9 shard_map.89
  104.1 13.4 %all_to_all.49.msg_ref = f32[32,8,128]{2,1,0:T(8,128)S(1)} all-to-all(f32[32,8,128]{2,1,0:T(8,128)S(1)} %get-tuple-element.38), channel_id=1, replica_groups=mesh['grp'=8,'tile'=32] {'tile'}, dimensions={0} | all-to-all | bytes 262144 | tf_op jit(solution)/shard_map/all_to_all | solution.py:367
  117.6 1.0 shard_map.90
  118.6 11.3 %all_to_all.50.msg_ref = f32[32,8,128]{2,1,0:T(8,128)S(1)} all-to-all(f32[32,8,128]{2,1,0:T(8,128)S(1)} %shard_map.90), channel_id=1, replica_groups=mesh['grp'=8,'tile'=32] {'tile'}, dimensions={0} | all-to-all | bytes 262144 | tf_op jit(solution)/shard_map/all_to_all | solution.py:367
  129.9 1.0 shard_map.91
  130.9 11.3 %all_to_all.51.msg_ref = f32[32,8,128]{2,1,0:T(8,128)S(1)} all-to-all(f32[32,8,128]{2,1,0:T(8,128)S(1)} %shard_map.91), channel_id=1, replica_groups=mesh['grp'=8,'tile'=32] {'tile'}, dimensions={0} | all-to-all | bytes 262144 | tf_op jit(solution)/shard_map/all_to_all | solution.py:367
  142.2 0.8 shard_map.92
  142.9 15.4 %all_to_all.52 = f32[32,33,1,128]{3,2,1,0:T(1,128)S(1)} all-to-all(f32[32,33,1,128]{3,2,1,0:T(1,128)S(1)} %bitcast.9), channel_id=1, replica_groups=mesh['grp'=8,'tile'=32] {'tile'}, dimensions={0} | all-to-all | bytes 1081344 | tf_op jit(solution)/shard_map/all_to_all | solution.py:367
  158.3 0.8 shard_map.93
  (16 shorter events, 0.1 us)
Async XLA Ops:
  6.8 9.3 %copy-start.3 = (f32[1,1024]{1,0:T(1,128)S(1)}, f32[1,1024]{1,0:T(1,128)}, u32[]{:S(2)}) copy-start(f32[1,1024]{1,0:T(1,128)} %param.13) | copy-start | bytes 12292
  6.8 10.0 %copy-start.1 = (f32[1,1024]{1,0:T(1,128)S(1)}, f32[1,1024]{1,0:T(1,128)}, u32[]{:S(2)}) copy-start(f32[1,1024]{1,0:T(1,128)} %col_ref.1) | copy-start | bytes 12292
  6.8 10.0 %copy-start.2 = (f32[128]{0:T(128)S(1)}, f32[128]{0:T(128)}, u32[]{:S(2)}) copy-start(f32[128]{0:T(128)} %param.14) | copy-start | bytes 1540
  6.8 27.1 %all-to-all-start = ((bf16[32,144,128]{2,1,0:T(8,128)(2,1)}), bf16[32,144,128]{2,1,0:T(8,128)(2,1)S(1)}, u32[]{:S(2)}, u32[]{:S(2)}) async-start(bf16[32,144,128]{2,1,0:T(8,128)(2,1)} %shard_map.82), calls=%async_computation | async-start | bytes 2359296 | tf_op jit(solution)/shard_map/all_to_all | solution.py:367
  33.9 19.9 %copy-start = (f32[128]{0:T(128)S(1)}, f32[128]{0:T(128)}, u32[]{:S(2)}) copy-start(f32[128]{0:T(128)} %param.15) | copy-start | bytes 1540
  55.9 16.8 %collective-permute-start.1 = (bf16[128,1024]{1,0:T(8,128)(2,1)S(1)}, bf16[128,1024]{1,0:T(8,128)(2,1)S(1)}, u32[]{:S(2)}, u32[]{:S(2)}) collective-permute-start(bf16[128,1024]{1,0:T(8,128)(2,1)S(1)} %get-tuple-element.26), channel_id=1, source_target_pairs={{0,224},{32,0},{64,32},{96,64},{128,96},{160,128},{192,160},{224,1... | collective-permute-start | bytes 786440 | tf_op jit(solution)/shard_map/ppermute | solution.py:435
  61.6 11.1 %collective-permute-start = (bf16[128,1024]{1,0:T(8,128)(2,1)S(1)}, bf16[128,1024]{1,0:T(8,128)(2,1)S(1)}, u32[]{:S(2)}, u32[]{:S(2)}) collective-permute-start(bf16[128,1024]{1,0:T(8,128)(2,1)S(1)} %get-tuple-element.26), channel_id=1, source_target_pairs={{0,32},{32,64},{64,96},{96,128},{128,160},{160,192},{192,224},{224... | collective-permute-start | bytes 786440 | tf_op jit(solution)/shard_map/ppermute | solution.py:434
  72.7 15.9 %collective-permute-start.2 = (bf16[128,1024]{1,0:T(8,128)(2,1)S(1)}, bf16[128,1024]{1,0:T(8,128)(2,1)S(1)}, u32[]{:S(2)}, u32[]{:S(2)}) collective-permute-start(bf16[128,1024]{1,0:T(8,128)(2,1)S(1)} %collective-permute-done.odd_ref.refs_1_), channel_id=1, source_target_pairs={{0,32},{32,64},{64,96},{96,128},{128,160},{160,192},{192,224},{224... | collective-permute-start | bytes 786440 | tf_op jit(solution)/shard_map/ppermute | solution.py:441
  73.0 15.6 %collective-permute-start.3 = (bf16[128,1024]{1,0:T(8,128)(2,1)S(1)}, bf16[128,1024]{1,0:T(8,128)(2,1)S(1)}, u32[]{:S(2)}, u32[]{:S(2)}) collective-permute-start(bf16[128,1024]{1,0:T(8,128)(2,1)S(1)} %collective-permute-done.1.even_ref.refs_7_), channel_id=1, source_target_pairs={{0,224},{32,0},{64,32},{96,64},{128,96},{160,128},{192,160},{224,1... | collective-permute-start | bytes 786440 | tf_op jit(solution)/shard_map/ppermute | solution.py:442
  75.4 16.0 %collective-permute-start.4 = (bf16[128,1024]{1,0:T(8,128)(2,1)S(1)}, bf16[128,1024]{1,0:T(8,128)(2,1)S(1)}, u32[]{:S(2)}, u32[]{:S(2)}) collective-permute-start(bf16[128,1024]{1,0:T(8,128)(2,1)S(1)} %shard_map.88), channel_id=1, source_target_pairs={{0,160},{1,97},{2,162},{3,99},{4,164},{5,101},{6,166},{7,103},{8,1... | collective-permute-start | bytes 786440 | tf_op jit(solution)/shard_map/ppermute | solution.py:452
  88.6 14.7 %collective-permute-start.5 = (bf16[128,1024]{1,0:T(8,128)(2,1)S(1)}, bf16[128,1024]{1,0:T(8,128)(2,1)S(1)}, u32[]{:S(2)}, u32[]{:S(2)}) collective-permute-start(bf16[128,1024]{1,0:T(8,128)(2,1)S(1)} %collective-permute-done.2.refs_2_), channel_id=1, source_target_pairs={{0,32},{32,64},{64,96},{96,128},{128,160},{160,192},{192,224},{224... | collective-permute-start | bytes 786440 | tf_op jit(solution)/shard_map/ppermute | solution.py:441
  88.9 14.3 %collective-permute-start.6 = (bf16[128,1024]{1,0:T(8,128)(2,1)S(1)}, bf16[128,1024]{1,0:T(8,128)(2,1)S(1)}, u32[]{:S(2)}, u32[]{:S(2)}) collective-permute-start(bf16[128,1024]{1,0:T(8,128)(2,1)S(1)} %collective-permute-done.3.refs_6_), channel_id=1, source_target_pairs={{0,224},{32,0},{64,32},{96,64},{128,96},{160,128},{192,160},{224,1... | collective-permute-start | bytes 786440 | tf_op jit(solution)/shard_map/ppermute | solution.py:442

commit v3 on v2

--- a/solution.py
+++ b/solution.py
@@ -184,9 +184,18 @@
     lax.fori_loop(0, HEAT_STEPS // 2, two_steps, 0)
     shift = lax.rem(lax.axis_index("tile") + 2, 4) * 32
     extra = mass + pltpu.roll(rcoef_ref[...], shift, 1)
-    for d in range(tiles):
-        out_ref[PART * d : PART * d + 32, :] = a_ref[8 + 32 * d : 40 + 32 * d, :]
-        out_ref[PART * d + 32 : PART * d + 33, :] = extra[d : d + 1, :]
+    sub = iota((8, LANES), 0)
+    for at in range(0, tiles * PART, 8):
+        d, row = at // PART, at % PART
+        start = 8 + 32 * d + row
+        block = a_ref[start : start + 8, :]
+        if row > 24:
+            place = 32 - row
+            after = a_ref[start - 1 : start + 7, :]
+            block = jnp.where(
+                sub < place, block, jnp.where(sub == place, extra[d : d + 1, :], after)
+            )
+        out_ref[at : at + 8, :] = block
 
 
 def tile_of(parts):

time: 160 us -> 160 us (level)
  no operation moved by 1% of the time
where the time goes in v3:
time: 160 us; the launch traced here: 159 us
  blocking collectives  103 us (64%)
  starting transfers between devices  19.8 us (12%)
  Pallas kernels  18.5 us (12%)
  waiting for transfers between devices  16.8 us (10%)
    all_to_all x8, blocking collectives, swap(): return lax.all_to_all(values, axis, split_axis=0, concat_axis=0, tiled=True)  103 us
    pallas_call x12, Pallas kernels, call(): pl.pallas_call(kernel, out_shape=out_shape, in_specs=specs, out_specs=out...  18.5 us
    all_to_all x1, waiting for transfers between devices, swap(): return lax.all_to_all(values, axis, split_axis=0, concat_axis=0, tiled=True)  16.7 us
    all_to_all x1, starting transfers between devices, swap(): return lax.all_to_all(values, axis, split_axis=0, concat_axis=0, tiled=True)  8.73 us
    ppermute x1, starting transfers between devices, body(): after = [kt, lax.ppermute(short, 'grp', down)]  5.65 us
    ppermute x2, starting transfers between devices, forward(): after.append(lax.ppermute(first, 'grp', down))  4.67 us
  transfers between devices with their start and end apart: 8, of which 1 were waited for; matrix products, arithmetic and copies ran while one was open for 1% of the time, Pallas kernels for 0%

profile of v3, /device:TPU:1, one launch (start us, length us, event | category | flops | bytes accessed | tf_op | source)
XLA Modules:
  0.0 159.2 jit_solution(11988559561176137213)
XLA Ops:
  0.0 6.8 %shard_map.82 = bf16[32,144,128]{2,1,0:T(8,128)(2,1)} custom-call(s32[1,2048]{1,0:T(1,128)} %bitcast.17, s32[1,2048]{1,0:T(1,128)} %bitcast.18, bf16[16,128]{1,0:T(8,128)(2,1)} %bitcast.19, bf16[2048,128]{1,0:T(8,128)(2,1)} %terms_hbm.1), custom_call_target="tpu_custom_call" | custom-call | tf_op jit(solution)/shard_map/pallas_call | solution.py:35
  6.8 0.0 copy-start.3
  6.8 0.0 copy-start.2
  6.8 8.7 %all-to-all-start = ((bf16[32,144,128]{2,1,0:T(8,128)(2,1)}), bf16[32,144,128]{2,1,0:T(8,128)(2,1)S(1)}, u32[]{:S(2)}, u32[]{:S(2)}) async-start(bf16[32,144,128]{2,1,0:T(8,128)(2,1)} %shard_map.82), calls=%async_computation | async-start | bytes 2359296 | tf_op jit(solution)/shard_map/all_to_all | solution.py:376
  15.6 0.5 broadcast.5
  16.1 0.7 reduce.3
  16.8 0.1 reshape.34
  16.8 0.3 shard_map.83
  17.2 16.7 %all-to-all-done.msg_ref = bf16[32,144,128]{2,1,0:T(8,128)(2,1)S(1)} async-done(((bf16[32,144,128]{2,1,0:T(8,128)(2,1)}), bf16[32,144,128]{2,1,0:T(8,128)(2,1)S(1)}, u32[]{:S(2)}, u32[]{:S(2)}) %all-to-all-start) | async-done | bytes 1179680 | tf_op jit(solution)/shard_map/all_to_all | solution.py:376
  33.9 4.4 %shard_map.84 = f32[1056,128]{1,0:T(8,128)S(1)} custom-call(bf16[32,144,128]{2,1,0:T(8,128)(2,1)S(1)} %all-to-all-done.msg_ref, f32[1024,128]{1,0:T(8,128)S(1)} %get-tuple-element.23.ccol_ref, f32[32,128]{1,0:T(8,128)S(1)} %pad.4.rcoef_ref), custom_call_target="tpu_custom_call" | custom-call | tf_op jit(solution)/shard_map/pallas_call | solution.py:35
  38.3 15.5 %all_to_all.45 = f32[32,33,1,128]{3,2,1,0:T(1,128)S(1)} all-to-all(f32[32,33,1,128]{3,2,1,0:T(1,128)S(1)} %bitcast.11), channel_id=1, replica_groups=mesh['grp'=8,'tile'=32] {'tile'}, dimensions={0} | all-to-all | bytes 1081344 | tf_op jit(solution)/shard_map/all_to_all | solution.py:376
  53.8 2.1 %shard_map.85 = (f32[128,1024]{1,0:T(8,128)S(1)}, bf16[128,1024]{1,0:T(8,128)(2,1)S(1)}, f32[8,128]{1,0:T(8,128)S(1)}, f32[8,16,128]{2,1,0:T(8,128)S(1)}) custom-call(f32[1056,128]{1,0:T(8,128)S(1)} %bitcast.10, f32[128,128]{1,0:T(8,128)S(1)} %get-tuple-element.24.patch_ref, f32[1,128]{1,0:T(1,128)S(1)} %bitcast.13), custom_call_target="tpu_custom_call" | custom-call | tf_op jit(solution)/shard_map/pallas_call | solution.py:35
  56.0 5.7 %collective-permute-start.1 = (bf16[128,1024]{1,0:T(8,128)(2,1)S(1)}, bf16[128,1024]{1,0:T(8,128)(2,1)S(1)}, u32[]{:S(2)}, u32[]{:S(2)}) collective-permute-start(bf16[128,1024]{1,0:T(8,128)(2,1)S(1)} %get-tuple-element.26), channel_id=1, source_target_pairs={{0,224},{32,0},{64,32},{96,64},{128,96},{160,128},{192,160},{224,1... | collective-permute-start | bytes 786440 | tf_op jit(solution)/shard_map/ppermute | solution.py:444
  61.6 11.0 %all_to_all.46.msg_ref = f32[8,16,128]{2,1,0:T(8,128)S(1)} all-to-all(f32[8,16,128]{2,1,0:T(8,128)S(1)} %get-tuple-element.25), channel_id=1, replica_groups=mesh['grp'=8,'tile'=32] {'grp'}, dimensions={0} | all-to-all | bytes 131072 | tf_op jit(solution)/shard_map/all_to_all | solution.py:376
  72.7 0.3 collective-permute-start.2
  73.0 2.4 %collective-permute-start.3 = (bf16[128,1024]{1,0:T(8,128)(2,1)S(1)}, bf16[128,1024]{1,0:T(8,128)(2,1)S(1)}, u32[]{:S(2)}, u32[]{:S(2)}) collective-permute-start(bf16[128,1024]{1,0:T(8,128)(2,1)S(1)} %collective-permute-done.1.even_ref.refs_7_), channel_id=1, source_target_pairs={{0,224},{32,0},{64,32},{96,64},{128,96},{160,128},{192,160},{224,1... | collective-permute-start | bytes 786440 | tf_op jit(solution)/shard_map/ppermute | solution.py:451
  75.4 0.1 collective-permute-start.4
  75.5 0.1 shard_map.86
  75.6 13.0 %all_to_all.47.msg_ref = f32[32,1,128]{2,1,0:T(1,128)S(1)} all-to-all(f32[32,1,128]{2,1,0:T(1,128)S(1)} %get-tuple-element.30), channel_id=1, replica_groups=mesh['grp'=8,'tile'=32] {'tile'}, dimensions={0} | all-to-all | bytes 32768 | tf_op jit(solution)/shard_map/all_to_all | solution.py:376
  88.6 0.4 collective-permute-start.5
  88.9 2.3 %collective-permute-start.6 = (bf16[128,1024]{1,0:T(8,128)(2,1)S(1)}, bf16[128,1024]{1,0:T(8,128)(2,1)S(1)}, u32[]{:S(2)}, u32[]{:S(2)}) collective-permute-start(bf16[128,1024]{1,0:T(8,128)(2,1)S(1)} %collective-permute-done.3.refs_6_), channel_id=1, source_target_pairs={{0,224},{32,0},{64,32},{96,64},{128,96},{160,128},{192,160},{224,1... | collective-permute-start | bytes 786440 | tf_op jit(solution)/shard_map/ppermute | solution.py:451
  91.3 0.1 shard_map.87
  91.4 11.8 %all_to_all.48.msg_ref = f32[8,16,128]{2,1,0:T(8,128)S(1)} all-to-all(f32[8,16,128]{2,1,0:T(8,128)S(1)} %shard_map.87), channel_id=1, replica_groups=mesh['grp'=8,'tile'=32] {'grp'}, dimensions={0} | all-to-all | bytes 131072 | tf_op jit(solution)/shard_map/all_to_all | solution.py:376
  103.2 0.9 shard_map.89
  104.2 13.4 %all_to_all.49.msg_ref = f32[32,8,128]{2,1,0:T(8,128)S(1)} all-to-all(f32[32,8,128]{2,1,0:T(8,128)S(1)} %get-tuple-element.38), channel_id=1, replica_groups=mesh['grp'=8,'tile'=32] {'tile'}, dimensions={0} | all-to-all | bytes 262144 | tf_op jit(solution)/shard_map/all_to_all | solution.py:376
  117.6 1.0 shard_map.90
  118.6 11.3 %all_to_all.50.msg_ref = f32[32,8,128]{2,1,0:T(8,128)S(1)} all-to-all(f32[32,8,128]{2,1,0:T(8,128)S(1)} %shard_map.90), channel_id=1, replica_groups=mesh['grp'=8,'tile'=32] {'tile'}, dimensions={0} | all-to-all | bytes 262144 | tf_op jit(solution)/shard_map/all_to_all | solution.py:376
  129.9 1.0 shard_map.91
  130.9 11.3 %all_to_all.51.msg_ref = f32[32,8,128]{2,1,0:T(8,128)S(1)} all-to-all(f32[32,8,128]{2,1,0:T(8,128)S(1)} %shard_map.91), channel_id=1, replica_groups=mesh['grp'=8,'tile'=32] {'tile'}, dimensions={0} | all-to-all | bytes 262144 | tf_op jit(solution)/shard_map/all_to_all | solution.py:376
  142.2 0.8 shard_map.92
  142.9 15.4 %all_to_all.52 = f32[32,33,1,128]{3,2,1,0:T(1,128)S(1)} all-to-all(f32[32,33,1,128]{3,2,1,0:T(1,128)S(1)} %bitcast.9), channel_id=1, replica_groups=mesh['grp'=8,'tile'=32] {'tile'}, dimensions={0} | all-to-all | bytes 1081344 | tf_op jit(solution)/shard_map/all_to_all | solution.py:376
  158.3 0.8 shard_map.93
  (16 shorter events, 0.1 us)
Async XLA Ops:
  6.8 9.3 %copy-start.3 = (f32[1,1024]{1,0:T(1,128)S(1)}, f32[1,1024]{1,0:T(1,128)}, u32[]{:S(2)}) copy-start(f32[1,1024]{1,0:T(1,128)} %param.13) | copy-start | bytes 12292
  6.8 10.0 %copy-start.1 = (f32[1,1024]{1,0:T(1,128)S(1)}, f32[1,1024]{1,0:T(1,128)}, u32[]{:S(2)}) copy-start(f32[1,1024]{1,0:T(1,128)} %col_ref.1) | copy-start | bytes 12292
  6.8 10.0 %copy-start.2 = (f32[128]{0:T(128)S(1)}, f32[128]{0:T(128)}, u32[]{:S(2)}) copy-start(f32[128]{0:T(128)} %param.14) | copy-start | bytes 1540
  6.8 27.1 %all-to-all-start = ((bf16[32,144,128]{2,1,0:T(8,128)(2,1)}), bf16[32,144,128]{2,1,0:T(8,128)(2,1)S(1)}, u32[]{:S(2)}, u32[]{:S(2)}) async-start(bf16[32,144,128]{2,1,0:T(8,128)(2,1)} %shard_map.82), calls=%async_computation | async-start | bytes 2359296 | tf_op jit(solution)/shard_map/all_to_all | solution.py:376
  33.9 19.9 %copy-start = (f32[128]{0:T(128)S(1)}, f32[128]{0:T(128)}, u32[]{:S(2)}) copy-start(f32[128]{0:T(128)} %param.15) | copy-start | bytes 1540
  56.0 16.7 %collective-permute-start.1 = (bf16[128,1024]{1,0:T(8,128)(2,1)S(1)}, bf16[128,1024]{1,0:T(8,128)(2,1)S(1)}, u32[]{:S(2)}, u32[]{:S(2)}) collective-permute-start(bf16[128,1024]{1,0:T(8,128)(2,1)S(1)} %get-tuple-element.26), channel_id=1, source_target_pairs={{0,224},{32,0},{64,32},{96,64},{128,96},{160,128},{192,160},{224,1... | collective-permute-start | bytes 786440 | tf_op jit(solution)/shard_map/ppermute | solution.py:444
  61.6 11.1 %collective-permute-start = (bf16[128,1024]{1,0:T(8,128)(2,1)S(1)}, bf16[128,1024]{1,0:T(8,128)(2,1)S(1)}, u32[]{:S(2)}, u32[]{:S(2)}) collective-permute-start(bf16[128,1024]{1,0:T(8,128)(2,1)S(1)} %get-tuple-element.26), channel_id=1, source_target_pairs={{0,32},{32,64},{64,96},{96,128},{128,160},{160,192},{192,224},{224... | collective-permute-start | bytes 786440 | tf_op jit(solution)/shard_map/ppermute | solution.py:443
  72.7 15.9 %collective-permute-start.2 = (bf16[128,1024]{1,0:T(8,128)(2,1)S(1)}, bf16[128,1024]{1,0:T(8,128)(2,1)S(1)}, u32[]{:S(2)}, u32[]{:S(2)}) collective-permute-start(bf16[128,1024]{1,0:T(8,128)(2,1)S(1)} %collective-permute-done.odd_ref.refs_1_), channel_id=1, source_target_pairs={{0,32},{32,64},{64,96},{96,128},{128,160},{160,192},{192,224},{224... | collective-permute-start | bytes 786440 | tf_op jit(solution)/shard_map/ppermute | solution.py:450
  73.0 15.6 %collective-permute-start.3 = (bf16[128,1024]{1,0:T(8,128)(2,1)S(1)}, bf16[128,1024]{1,0:T(8,128)(2,1)S(1)}, u32[]{:S(2)}, u32[]{:S(2)}) collective-permute-start(bf16[128,1024]{1,0:T(8,128)(2,1)S(1)} %collective-permute-done.1.even_ref.refs_7_), channel_id=1, source_target_pairs={{0,224},{32,0},{64,32},{96,64},{128,96},{160,128},{192,160},{224,1... | collective-permute-start | bytes 786440 | tf_op jit(solution)/shard_map/ppermute | solution.py:451
  75.4 16.0 %collective-permute-start.4 = (bf16[128,1024]{1,0:T(8,128)(2,1)S(1)}, bf16[128,1024]{1,0:T(8,128)(2,1)S(1)}, u32[]{:S(2)}, u32[]{:S(2)}) collective-permute-start(bf16[128,1024]{1,0:T(8,128)(2,1)S(1)} %shard_map.88), channel_id=1, source_target_pairs={{0,160},{1,97},{2,162},{3,99},{4,164},{5,101},{6,166},{7,103},{8,1... | collective-permute-start | bytes 786440 | tf_op jit(solution)/shard_map/ppermute | solution.py:461
  88.6 14.7 %collective-permute-start.5 = (bf16[128,1024]{1,0:T(8,128)(2,1)S(1)}, bf16[128,1024]{1,0:T(8,128)(2,1)S(1)}, u32[]{:S(2)}, u32[]{:S(2)}) collective-permute-start(bf16[128,1024]{1,0:T(8,128)(2,1)S(1)} %collective-permute-done.2.refs_2_), channel_id=1, source_target_pairs={{0,32},{32,64},{64,96},{96,128},{128,160},{160,192},{192,224},{224... | collective-permute-start | bytes 786440 | tf_op jit(solution)/shard_map/ppermute | solution.py:450
  88.9 14.3 %collective-permute-start.6 = (bf16[128,1024]{1,0:T(8,128)(2,1)S(1)}, bf16[128,1024]{1,0:T(8,128)(2,1)S(1)}, u32[]{:S(2)}, u32[]{:S(2)}) collective-permute-start(bf16[128,1024]{1,0:T(8,128)(2,1)S(1)} %collective-permute-done.3.refs_6_), channel_id=1, source_target_pairs={{0,224},{32,0},{64,32},{96,64},{128,96},{160,128},{192,160},{224,1... | collective-permute-start | bytes 786440 | tf_op jit(solution)/shard_map/ppermute | solution.py:451

commit v4 on v3

--- a/solution.py
+++ b/solution.py
@@ -182,8 +182,8 @@
         return carry
 
     lax.fori_loop(0, HEAT_STEPS // 2, two_steps, 0)
-    shift = lax.rem(lax.axis_index("tile") + 2, 4) * 32
-    extra = mass + pltpu.roll(rcoef_ref[...], shift, 1)
+    quarter = lax.rem(lax.axis_index("tile"), 4)
+    extra = jnp.where(iota((tiles, LANES), 1) // 32 == quarter, mass, rcoef_ref[...])
     sub = iota((8, LANES), 0)
     for at in range(0, tiles * PART, 8):
         d, row = at // PART, at % PART
@@ -416,7 +416,7 @@
         (shape((cells, LANES), F32), shape((LANES, LANES), F32)),
         [col_coef, tgt_coef.reshape(1, columns)],
     )
-    rcoef = jnp.pad(row_coef.reshape(tiles, 32), ((0, 0), (0, LANES - 32)))
+    rcoef = jnp.tile(row_coef.reshape(tiles, 32), (1, LANES // 32))
     got = swap(packed, "tile")
     sorted_field = call(
         gather_kernel,

time: 160 us -> 159 us (level)
  no operation moved by 1% of the time
where the time goes in v4:
time: 159 us
  blocking collectives  103 us (65%)
  starting transfers between devices  19.8 us (12%)
  Pallas kernels  17.9 us (11%)
  waiting for transfers between devices  16.6 us (10%)
    all_to_all x8, blocking collectives, swap(): return lax.all_to_all(values, axis, split_axis=0, concat_axis=0, tiled=True)  103 us
    pallas_call x12, Pallas kernels, call(): pl.pallas_call(kernel, out_shape=out_shape, in_specs=specs, out_specs=out...  17.9 us
    all_to_all x1, waiting for transfers between devices, swap(): return lax.all_to_all(values, axis, split_axis=0, concat_axis=0, tiled=True)  16.6 us
    all_to_all x1, starting transfers between devices, swap(): return lax.all_to_all(values, axis, split_axis=0, concat_axis=0, tiled=True)  8.73 us
    ppermute x1, starting transfers between devices, body(): after = [kt, lax.ppermute(short, 'grp', down)]  5.65 us
    ppermute x2, starting transfers between devices, forward(): after.append(lax.ppermute(first, 'grp', down))  4.71 us
  transfers between devices with their start and end apart: 8, of which 1 were waited for; matrix products, arithmetic and copies ran while one was open for 1% of the time, Pallas kernels for 0%

profile of v4, /device:TPU:1, one launch (start us, length us, event | category | flops | bytes accessed | tf_op | source)
XLA Modules:
  0.0 158.6 jit_solution(13142947586731077906)
XLA Ops:
  0.0 6.8 %shard_map.82 = bf16[32,144,128]{2,1,0:T(8,128)(2,1)} custom-call(s32[1,2048]{1,0:T(1,128)} %bitcast.17, s32[1,2048]{1,0:T(1,128)} %bitcast.18, bf16[16,128]{1,0:T(8,128)(2,1)} %bitcast.19, bf16[2048,128]{1,0:T(8,128)(2,1)} %terms_hbm.1), custom_call_target="tpu_custom_call" | custom-call | tf_op jit(solution)/shard_map/pallas_call | solution.py:35
  6.8 0.0 copy-start.3
  6.8 8.7 %all-to-all-start = ((bf16[32,144,128]{2,1,0:T(8,128)(2,1)}), bf16[32,144,128]{2,1,0:T(8,128)(2,1)S(1)}, u32[]{:S(2)}, u32[]{:S(2)}) async-start(bf16[32,144,128]{2,1,0:T(8,128)(2,1)} %shard_map.82), calls=%async_computation | async-start | bytes 2359296 | tf_op jit(solution)/shard_map/all_to_all | solution.py:376
  15.6 0.5 broadcast.5
  16.1 0.7 reduce.3
  16.8 0.1 tile.10
  16.8 0.1 tile.12.rcoef_ref
  17.0 0.3 shard_map.83
  17.3 16.6 %all-to-all-done.msg_ref = bf16[32,144,128]{2,1,0:T(8,128)(2,1)S(1)} async-done(((bf16[32,144,128]{2,1,0:T(8,128)(2,1)}), bf16[32,144,128]{2,1,0:T(8,128)(2,1)S(1)}, u32[]{:S(2)}, u32[]{:S(2)}) %all-to-all-start) | async-done | bytes 1179680 | tf_op jit(solution)/shard_map/all_to_all | solution.py:376
  33.9 3.8 %shard_map.84 = f32[1056,128]{1,0:T(8,128)S(1)} custom-call(bf16[32,144,128]{2,1,0:T(8,128)(2,1)S(1)} %all-to-all-done.msg_ref, f32[1024,128]{1,0:T(8,128)S(1)} %get-tuple-element.23.ccol_ref, f32[32,128]{1,0:T(8,128)S(1)} %tile.12.rcoef_ref), custom_call_target="tpu_custom_call" | custom-call | tf_op jit(solution)/shard_map/pallas_call | solution.py:35
  37.8 15.5 %all_to_all.45 = f32[32,33,1,128]{3,2,1,0:T(1,128)S(1)} all-to-all(f32[32,33,1,128]{3,2,1,0:T(1,128)S(1)} %bitcast.11), channel_id=1, replica_groups=mesh['grp'=8,'tile'=32] {'tile'}, dimensions={0} | all-to-all | bytes 1081344 | tf_op jit(solution)/shard_map/all_to_all | solution.py:376
  53.3 2.1 %shard_map.85 = (f32[128,1024]{1,0:T(8,128)S(1)}, bf16[128,1024]{1,0:T(8,128)(2,1)S(1)}, f32[8,128]{1,0:T(8,128)S(1)}, f32[8,16,128]{2,1,0:T(8,128)S(1)}) custom-call(f32[1056,128]{1,0:T(8,128)S(1)} %bitcast.10, f32[128,128]{1,0:T(8,128)S(1)} %get-tuple-element.24.patch_ref, f32[1,128]{1,0:T(1,128)S(1)} %bitcast.13), custom_call_target="tpu_custom_call" | custom-call | tf_op jit(solution)/shard_map/pallas_call | solution.py:35
  55.4 5.7 %collective-permute-start.1 = (bf16[128,1024]{1,0:T(8,128)(2,1)S(1)}, bf16[128,1024]{1,0:T(8,128)(2,1)S(1)}, u32[]{:S(2)}, u32[]{:S(2)}) collective-permute-start(bf16[128,1024]{1,0:T(8,128)(2,1)S(1)} %get-tuple-element.26), channel_id=1, source_target_pairs={{0,224},{32,0},{64,32},{96,64},{128,96},{160,128},{192,160},{224,1... | collective-permute-start | bytes 786440 | tf_op jit(solution)/shard_map/ppermute | solution.py:444
  61.0 11.1 %all_to_all.46.msg_ref = f32[8,16,128]{2,1,0:T(8,128)S(1)} all-to-all(f32[8,16,128]{2,1,0:T(8,128)S(1)} %get-tuple-element.25), channel_id=1, replica_groups=mesh['grp'=8,'tile'=32] {'grp'}, dimensions={0} | all-to-all | bytes 131072 | tf_op jit(solution)/shard_map/all_to_all | solution.py:376
  72.2 0.3 collective-permute-start.2
  72.4 2.4 %collective-permute-start.3 = (bf16[128,1024]{1,0:T(8,128)(2,1)S(1)}, bf16[128,1024]{1,0:T(8,128)(2,1)S(1)}, u32[]{:S(2)}, u32[]{:S(2)}) collective-permute-start(bf16[128,1024]{1,0:T(8,128)(2,1)S(1)} %collective-permute-done.1.even_ref.refs_7_), channel_id=1, source_target_pairs={{0,224},{32,0},{64,32},{96,64},{128,96},{160,128},{192,160},{224,1... | collective-permute-start | bytes 786440 | tf_op jit(solution)/shard_map/ppermute | solution.py:451
  74.9 0.1 collective-permute-start.4
  74.9 0.1 shard_map.86
  75.1 12.9 %all_to_all.47.msg_ref = f32[32,1,128]{2,1,0:T(1,128)S(1)} all-to-all(f32[32,1,128]{2,1,0:T(1,128)S(1)} %get-tuple-element.30), channel_id=1, replica_groups=mesh['grp'=8,'tile'=32] {'tile'}, dimensions={0} | all-to-all | bytes 32768 | tf_op jit(solution)/shard_map/all_to_all | solution.py:376
  88.0 0.4 collective-permute-start.5
  88.4 2.3 %collective-permute-start.6 = (bf16[128,1024]{1,0:T(8,128)(2,1)S(1)}, bf16[128,1024]{1,0:T(8,128)(2,1)S(1)}, u32[]{:S(2)}, u32[]{:S(2)}) collective-permute-start(bf16[128,1024]{1,0:T(8,128)(2,1)S(1)} %collective-permute-done.3.refs_6_), channel_id=1, source_target_pairs={{0,224},{32,0},{64,32},{96,64},{128,96},{160,128},{192,160},{224,1... | collective-permute-start | bytes 786440 | tf_op jit(solution)/shard_map/ppermute | solution.py:451
  90.7 0.1 shard_map.87
  90.8 11.8 %all_to_all.48.msg_ref = f32[8,16,128]{2,1,0:T(8,128)S(1)} all-to-all(f32[8,16,128]{2,1,0:T(8,128)S(1)} %shard_map.87), channel_id=1, replica_groups=mesh['grp'=8,'tile'=32] {'grp'}, dimensions={0} | all-to-all | bytes 131072 | tf_op jit(solution)/shard_map/all_to_all | solution.py:376
  102.7 0.9 shard_map.89
  103.6 13.4 %all_to_all.49.msg_ref = f32[32,8,128]{2,1,0:T(8,128)S(1)} all-to-all(f32[32,8,128]{2,1,0:T(8,128)S(1)} %get-tuple-element.38), channel_id=1, replica_groups=mesh['grp'=8,'tile'=32] {'tile'}, dimensions={0} | all-to-all | bytes 262144 | tf_op jit(solution)/shard_map/all_to_all | solution.py:376
  117.0 1.0 shard_map.90
  118.0 11.3 %all_to_all.50.msg_ref = f32[32,8,128]{2,1,0:T(8,128)S(1)} all-to-all(f32[32,8,128]{2,1,0:T(8,128)S(1)} %shard_map.90), channel_id=1, replica_groups=mesh['grp'=8,'tile'=32] {'tile'}, dimensions={0} | all-to-all | bytes 262144 | tf_op jit(solution)/shard_map/all_to_all | solution.py:376
  129.3 1.0 shard_map.91
  130.3 11.3 %all_to_all.51.msg_ref = f32[32,8,128]{2,1,0:T(8,128)S(1)} all-to-all(f32[32,8,128]{2,1,0:T(8,128)S(1)} %shard_map.91), channel_id=1, replica_groups=mesh['grp'=8,'tile'=32] {'tile'}, dimensions={0} | all-to-all | bytes 262144 | tf_op jit(solution)/shard_map/all_to_all | solution.py:376
  141.6 0.8 shard_map.92
  142.4 15.4 %all_to_all.52 = f32[32,33,1,128]{3,2,1,0:T(1,128)S(1)} all-to-all(f32[32,33,1,128]{3,2,1,0:T(1,128)S(1)} %bitcast.9), channel_id=1, replica_groups=mesh['grp'=8,'tile'=32] {'tile'}, dimensions={0} | all-to-all | bytes 1081344 | tf_op jit(solution)/shard_map/all_to_all | solution.py:376
  157.7 0.8 shard_map.93
  (17 shorter events, 0.1 us)
Async XLA Ops:
  6.8 9.3 %copy-start.3 = (f32[1,1024]{1,0:T(1,128)S(1)}, f32[1,1024]{1,0:T(1,128)}, u32[]{:S(2)}) copy-start(f32[1,1024]{1,0:T(1,128)} %param.13) | copy-start | bytes 12292
  6.8 10.1 %copy-start.1 = (f32[1,1024]{1,0:T(1,128)S(1)}, f32[1,1024]{1,0:T(1,128)}, u32[]{:S(2)}) copy-start(f32[1,1024]{1,0:T(1,128)} %col_ref.1) | copy-start | bytes 12292
  6.8 10.1 %copy-start.2 = (f32[128]{0:T(128)S(1)}, f32[128]{0:T(128)}, u32[]{:S(2)}) copy-start(f32[128]{0:T(128)} %param.14) | copy-start | bytes 1540
  6.8 27.1 %all-to-all-start = ((bf16[32,144,128]{2,1,0:T(8,128)(2,1)}), bf16[32,144,128]{2,1,0:T(8,128)(2,1)S(1)}, u32[]{:S(2)}, u32[]{:S(2)}) async-start(bf16[32,144,128]{2,1,0:T(8,128)(2,1)} %shard_map.82), calls=%async_computation | async-start | bytes 2359296 | tf_op jit(solution)/shard_map/all_to_all | solution.py:376
  33.9 19.3 %copy-start = (f32[128]{0:T(128)S(1)}, f32[128]{0:T(128)}, u32[]{:S(2)}) copy-start(f32[128]{0:T(128)} %param.15) | copy-start | bytes 1540
  55.4 16.8 %collective-permute-start.1 = (bf16[128,1024]{1,0:T(8,128)(2,1)S(1)}, bf16[128,1024]{1,0:T(8,128)(2,1)S(1)}, u32[]{:S(2)}, u32[]{:S(2)}) collective-permute-start(bf16[128,1024]{1,0:T(8,128)(2,1)S(1)} %get-tuple-element.26), channel_id=1, source_target_pairs={{0,224},{32,0},{64,32},{96,64},{128,96},{160,128},{192,160},{224,1... | collective-permute-start | bytes 786440 | tf_op jit(solution)/shard_map/ppermute | solution.py:444
  61.0 11.1 %collective-permute-start = (bf16[128,1024]{1,0:T(8,128)(2,1)S(1)}, bf16[128,1024]{1,0:T(8,128)(2,1)S(1)}, u32[]{:S(2)}, u32[]{:S(2)}) collective-permute-start(bf16[128,1024]{1,0:T(8,128)(2,1)S(1)} %get-tuple-element.26), channel_id=1, source_target_pairs={{0,32},{32,64},{64,96},{96,128},{128,160},{160,192},{192,224},{224... | collective-permute-start | bytes 786440 | tf_op jit(solution)/shard_map/ppermute | solution.py:443
  72.2 15.9 %collective-permute-start.2 = (bf16[128,1024]{1,0:T(8,128)(2,1)S(1)}, bf16[128,1024]{1,0:T(8,128)(2,1)S(1)}, u32[]{:S(2)}, u32[]{:S(2)}) collective-permute-start(bf16[128,1024]{1,0:T(8,128)(2,1)S(1)} %collective-permute-done.odd_ref.refs_1_), channel_id=1, source_target_pairs={{0,32},{32,64},{64,96},{96,128},{128,160},{160,192},{192,224},{224... | collective-permute-start | bytes 786440 | tf_op jit(solution)/shard_map/ppermute | solution.py:450
  72.4 15.6 %collective-permute-start.3 = (bf16[128,1024]{1,0:T(8,128)(2,1)S(1)}, bf16[128,1024]{1,0:T(8,128)(2,1)S(1)}, u32[]{:S(2)}, u32[]{:S(2)}) collective-permute-start(bf16[128,1024]{1,0:T(8,128)(2,1)S(1)} %collective-permute-done.1.even_ref.refs_7_), channel_id=1, source_target_pairs={{0,224},{32,0},{64,32},{96,64},{128,96},{160,128},{192,160},{224,1... | collective-permute-start | bytes 786440 | tf_op jit(solution)/shard_map/ppermute | solution.py:451
  74.9 16.0 %collective-permute-start.4 = (bf16[128,1024]{1,0:T(8,128)(2,1)S(1)}, bf16[128,1024]{1,0:T(8,128)(2,1)S(1)}, u32[]{:S(2)}, u32[]{:S(2)}) collective-permute-start(bf16[128,1024]{1,0:T(8,128)(2,1)S(1)} %shard_map.88), channel_id=1, source_target_pairs={{0,160},{1,97},{2,162},{3,99},{4,164},{5,101},{6,166},{7,103},{8,1... | collective-permute-start | bytes 786440 | tf_op jit(solution)/shard_map/ppermute | solution.py:461
  88.0 14.7 %collective-permute-start.5 = (bf16[128,1024]{1,0:T(8,128)(2,1)S(1)}, bf16[128,1024]{1,0:T(8,128)(2,1)S(1)}, u32[]{:S(2)}, u32[]{:S(2)}) collective-permute-start(bf16[128,1024]{1,0:T(8,128)(2,1)S(1)} %collective-permute-done.2.refs_2_), channel_id=1, source_target_pairs={{0,32},{32,64},{64,96},{96,128},{128,160},{160,192},{192,224},{224... | collective-permute-start | bytes 786440 | tf_op jit(solution)/shard_map/ppermute | solution.py:450
  88.4 14.3 %collective-permute-start.6 = (bf16[128,1024]{1,0:T(8,128)(2,1)S(1)}, bf16[128,1024]{1,0:T(8,128)(2,1)S(1)}, u32[]{:S(2)}, u32[]{:S(2)}) collective-permute-start(bf16[128,1024]{1,0:T(8,128)(2,1)S(1)} %collective-permute-done.3.refs_6_), channel_id=1, source_target_pairs={{0,224},{32,0},{64,32},{96,64},{128,96},{160,128},{192,160},{224,1... | collective-permute-start | bytes 786440 | tf_op jit(solution)/shard_map/ppermute | solution.py:451

commit v5 on v4

--- a/solution.py
+++ b/solution.py
@@ -17,6 +17,7 @@
 PART = 33
 F32 = jnp.float32
 BF16 = jnp.bfloat16
+BF16_MAX = float(jnp.finfo(jnp.bfloat16).max)
 NT = (((1,), (1,)), ((), ()))
 EXACT = lax.Precision.HIGHEST
 
@@ -256,7 +257,7 @@
     )
     kernel = jnp.exp(EXPONENT_GAIN * smooth)
     kt_ref[...] = kernel
-    short_ref[...] = kernel.astype(BF16)
+    short_ref[...] = jnp.minimum(kernel, BF16_MAX).astype(BF16)
     tile = row_partials(kt_ref, None)
     for g in range(out_ref.shape[0]):
         out_ref[g, 0:8, :] = tile

time: 159 us -> 159 us (level)
  no operation moved by 1% of the time
where the time goes in v5:
time: 159 us
  blocking collectives  103 us (65%)
  starting transfers between devices  19.8 us (12%)
  Pallas kernels  17.9 us (11%)
  waiting for transfers between devices  16.6 us (10%)
    all_to_all x8, blocking collectives, swap(): return lax.all_to_all(values, axis, split_axis=0, concat_axis=0, tiled=True)  103 us
    pallas_call x12, Pallas kernels, call(): pl.pallas_call(kernel, out_shape=out_shape, in_specs=specs, out_specs=out...  17.9 us
    all_to_all x1, waiting for transfers between devices, swap(): return lax.all_to_all(values, axis, split_axis=0, concat_axis=0, tiled=True)  16.6 us
    all_to_all x1, starting transfers between devices, swap(): return lax.all_to_all(values, axis, split_axis=0, concat_axis=0, tiled=True)  8.73 us
    ppermute x1, starting transfers between devices, body(): after = [kt, lax.ppermute(short, 'grp', down)]  5.65 us
    ppermute x2, starting transfers between devices, forward(): after.append(lax.ppermute(first, 'grp', down))  4.71 us
  transfers between devices with their start and end apart: 8, of which 1 were waited for; matrix products, arithmetic and copies ran while one was open for 1% of the time, Pallas kernels for 0%

profile of v5, /device:TPU:1, one launch (start us, length us, event | category | flops | bytes accessed | tf_op | source)
XLA Modules:
  0.0 158.6 jit_solution(10728445128359714350)
XLA Ops:
  0.0 6.8 %shard_map.82 = bf16[32,144,128]{2,1,0:T(8,128)(2,1)} custom-call(s32[1,2048]{1,0:T(1,128)} %bitcast.17, s32[1,2048]{1,0:T(1,128)} %bitcast.18, bf16[16,128]{1,0:T(8,128)(2,1)} %bitcast.19, bf16[2048,128]{1,0:T(8,128)(2,1)} %terms_hbm.1), custom_call_target="tpu_custom_call" | custom-call | tf_op jit(solution)/shard_map/pallas_call | solution.py:36
  6.8 0.0 copy-start.3
  6.8 8.7 %all-to-all-start = ((bf16[32,144,128]{2,1,0:T(8,128)(2,1)}), bf16[32,144,128]{2,1,0:T(8,128)(2,1)S(1)}, u32[]{:S(2)}, u32[]{:S(2)}) async-start(bf16[32,144,128]{2,1,0:T(8,128)(2,1)} %shard_map.82), calls=%async_computation | async-start | bytes 2359296 | tf_op jit(solution)/shard_map/all_to_all | solution.py:377
  15.6 0.5 broadcast.5
  16.1 0.7 reduce.3
  16.8 0.1 tile.10
  16.8 0.1 tile.12.rcoef_ref
  17.0 0.3 shard_map.83
  17.3 16.6 %all-to-all-done.msg_ref = bf16[32,144,128]{2,1,0:T(8,128)(2,1)S(1)} async-done(((bf16[32,144,128]{2,1,0:T(8,128)(2,1)}), bf16[32,144,128]{2,1,0:T(8,128)(2,1)S(1)}, u32[]{:S(2)}, u32[]{:S(2)}) %all-to-all-start) | async-done | bytes 1179680 | tf_op jit(solution)/shard_map/all_to_all | solution.py:377
  33.9 3.8 %shard_map.84 = f32[1056,128]{1,0:T(8,128)S(1)} custom-call(bf16[32,144,128]{2,1,0:T(8,128)(2,1)S(1)} %all-to-all-done.msg_ref, f32[1024,128]{1,0:T(8,128)S(1)} %get-tuple-element.23.ccol_ref, f32[32,128]{1,0:T(8,128)S(1)} %tile.12.rcoef_ref), custom_call_target="tpu_custom_call" | custom-call | tf_op jit(solution)/shard_map/pallas_call | solution.py:36
  37.8 15.5 %all_to_all.45 = f32[32,33,1,128]{3,2,1,0:T(1,128)S(1)} all-to-all(f32[32,33,1,128]{3,2,1,0:T(1,128)S(1)} %bitcast.11), channel_id=1, replica_groups=mesh['grp'=8,'tile'=32] {'tile'}, dimensions={0} | all-to-all | bytes 1081344 | tf_op jit(solution)/shard_map/all_to_all | solution.py:377
  53.3 2.1 %shard_map.85 = (f32[128,1024]{1,0:T(8,128)S(1)}, bf16[128,1024]{1,0:T(8,128)(2,1)S(1)}, f32[8,128]{1,0:T(8,128)S(1)}, f32[8,16,128]{2,1,0:T(8,128)S(1)}) custom-call(f32[1056,128]{1,0:T(8,128)S(1)} %bitcast.10, f32[128,128]{1,0:T(8,128)S(1)} %get-tuple-element.24.patch_ref, f32[1,128]{1,0:T(1,128)S(1)} %bitcast.13), custom_call_target="tpu_custom_call" | custom-call | tf_op jit(solution)/shard_map/pallas_call | solution.py:36
  55.4 5.7 %collective-permute-start.1 = (bf16[128,1024]{1,0:T(8,128)(2,1)S(1)}, bf16[128,1024]{1,0:T(8,128)(2,1)S(1)}, u32[]{:S(2)}, u32[]{:S(2)}) collective-permute-start(bf16[128,1024]{1,0:T(8,128)(2,1)S(1)} %get-tuple-element.26), channel_id=1, source_target_pairs={{0,224},{32,0},{64,32},{96,64},{128,96},{160,128},{192,160},{224,1... | collective-permute-start | bytes 786440 | tf_op jit(solution)/shard_map/ppermute | solution.py:445
  61.1 11.1 %all_to_all.46.msg_ref = f32[8,16,128]{2,1,0:T(8,128)S(1)} all-to-all(f32[8,16,128]{2,1,0:T(8,128)S(1)} %get-tuple-element.25), channel_id=1, replica_groups=mesh['grp'=8,'tile'=32] {'grp'}, dimensions={0} | all-to-all | bytes 131072 | tf_op jit(solution)/shard_map/all_to_all | solution.py:377
  72.2 0.3 collective-permute-start.2
  72.4 2.4 %collective-permute-start.3 = (bf16[128,1024]{1,0:T(8,128)(2,1)S(1)}, bf16[128,1024]{1,0:T(8,128)(2,1)S(1)}, u32[]{:S(2)}, u32[]{:S(2)}) collective-permute-start(bf16[128,1024]{1,0:T(8,128)(2,1)S(1)} %collective-permute-done.1.even_ref.refs_7_), channel_id=1, source_target_pairs={{0,224},{32,0},{64,32},{96,64},{128,96},{160,128},{192,160},{224,1... | collective-permute-start | bytes 786440 | tf_op jit(solution)/shard_map/ppermute | solution.py:452
  74.9 0.1 collective-permute-start.4
  75.0 0.1 shard_map.86
  75.1 12.9 %all_to_all.47.msg_ref = f32[32,1,128]{2,1,0:T(1,128)S(1)} all-to-all(f32[32,1,128]{2,1,0:T(1,128)S(1)} %get-tuple-element.30), channel_id=1, replica_groups=mesh['grp'=8,'tile'=32] {'tile'}, dimensions={0} | all-to-all | bytes 32768 | tf_op jit(solution)/shard_map/all_to_all | solution.py:377
  88.0 0.4 collective-permute-start.5
  88.4 2.3 %collective-permute-start.6 = (bf16[128,1024]{1,0:T(8,128)(2,1)S(1)}, bf16[128,1024]{1,0:T(8,128)(2,1)S(1)}, u32[]{:S(2)}, u32[]{:S(2)}) collective-permute-start(bf16[128,1024]{1,0:T(8,128)(2,1)S(1)} %collective-permute-done.3.refs_6_), channel_id=1, source_target_pairs={{0,224},{32,0},{64,32},{96,64},{128,96},{160,128},{192,160},{224,1... | collective-permute-start | bytes 786440 | tf_op jit(solution)/shard_map/ppermute | solution.py:452
  90.7 0.1 shard_map.87
  90.8 11.8 %all_to_all.48.msg_ref = f32[8,16,128]{2,1,0:T(8,128)S(1)} all-to-all(f32[8,16,128]{2,1,0:T(8,128)S(1)} %shard_map.87), channel_id=1, replica_groups=mesh['grp'=8,'tile'=32] {'grp'}, dimensions={0} | all-to-all | bytes 131072 | tf_op jit(solution)/shard_map/all_to_all | solution.py:377
  102.7 0.9 shard_map.89
  103.6 13.4 %all_to_all.49.msg_ref = f32[32,8,128]{2,1,0:T(8,128)S(1)} all-to-all(f32[32,8,128]{2,1,0:T(8,128)S(1)} %get-tuple-element.38), channel_id=1, replica_groups=mesh['grp'=8,'tile'=32] {'tile'}, dimensions={0} | all-to-all | bytes 262144 | tf_op jit(solution)/shard_map/all_to_all | solution.py:377
  117.0 1.0 shard_map.90
  118.0 11.3 %all_to_all.50.msg_ref = f32[32,8,128]{2,1,0:T(8,128)S(1)} all-to-all(f32[32,8,128]{2,1,0:T(8,128)S(1)} %shard_map.90), channel_id=1, replica_groups=mesh['grp'=8,'tile'=32] {'tile'}, dimensions={0} | all-to-all | bytes 262144 | tf_op jit(solution)/shard_map/all_to_all | solution.py:377
  129.3 1.0 shard_map.91
  130.3 11.3 %all_to_all.51.msg_ref = f32[32,8,128]{2,1,0:T(8,128)S(1)} all-to-all(f32[32,8,128]{2,1,0:T(8,128)S(1)} %shard_map.91), channel_id=1, replica_groups=mesh['grp'=8,'tile'=32] {'tile'}, dimensions={0} | all-to-all | bytes 262144 | tf_op jit(solution)/shard_map/all_to_all | solution.py:377
  141.6 0.8 shard_map.92
  142.4 15.4 %all_to_all.52 = f32[32,33,1,128]{3,2,1,0:T(1,128)S(1)} all-to-all(f32[32,33,1,128]{3,2,1,0:T(1,128)S(1)} %bitcast.9), channel_id=1, replica_groups=mesh['grp'=8,'tile'=32] {'tile'}, dimensions={0} | all-to-all | bytes 1081344 | tf_op jit(solution)/shard_map/all_to_all | solution.py:377
  157.7 0.8 shard_map.93
  (17 shorter events, 0.1 us)
Async XLA Ops:
  6.8 9.3 %copy-start.3 = (f32[1,1024]{1,0:T(1,128)S(1)}, f32[1,1024]{1,0:T(1,128)}, u32[]{:S(2)}) copy-start(f32[1,1024]{1,0:T(1,128)} %param.13) | copy-start | bytes 12292
  6.8 10.1 %copy-start.1 = (f32[1,1024]{1,0:T(1,128)S(1)}, f32[1,1024]{1,0:T(1,128)}, u32[]{:S(2)}) copy-start(f32[1,1024]{1,0:T(1,128)} %col_ref.1) | copy-start | bytes 12292
  6.8 10.1 %copy-start.2 = (f32[128]{0:T(128)S(1)}, f32[128]{0:T(128)}, u32[]{:S(2)}) copy-start(f32[128]{0:T(128)} %param.14) | copy-start | bytes 1540
  6.8 27.1 %all-to-all-start = ((bf16[32,144,128]{2,1,0:T(8,128)(2,1)}), bf16[32,144,128]{2,1,0:T(8,128)(2,1)S(1)}, u32[]{:S(2)}, u32[]{:S(2)}) async-start(bf16[32,144,128]{2,1,0:T(8,128)(2,1)} %shard_map.82), calls=%async_computation | async-start | bytes 2359296 | tf_op jit(solution)/shard_map/all_to_all | solution.py:377
  33.9 19.3 %copy-start = (f32[128]{0:T(128)S(1)}, f32[128]{0:T(128)}, u32[]{:S(2)}) copy-start(f32[128]{0:T(128)} %param.15) | copy-start | bytes 1540
  55.4 16.8 %collective-permute-start.1 = (bf16[128,1024]{1,0:T(8,128)(2,1)S(1)}, bf16[128,1024]{1,0:T(8,128)(2,1)S(1)}, u32[]{:S(2)}, u32[]{:S(2)}) collective-permute-start(bf16[128,1024]{1,0:T(8,128)(2,1)S(1)} %get-tuple-element.26), channel_id=1, source_target_pairs={{0,224},{32,0},{64,32},{96,64},{128,96},{160,128},{192,160},{224,1... | collective-permute-start | bytes 786440 | tf_op jit(solution)/shard_map/ppermute | solution.py:445
  61.0 11.1 %collective-permute-start = (bf16[128,1024]{1,0:T(8,128)(2,1)S(1)}, bf16[128,1024]{1,0:T(8,128)(2,1)S(1)}, u32[]{:S(2)}, u32[]{:S(2)}) collective-permute-start(bf16[128,1024]{1,0:T(8,128)(2,1)S(1)} %get-tuple-element.26), channel_id=1, source_target_pairs={{0,32},{32,64},{64,96},{96,128},{128,160},{160,192},{192,224},{224... | collective-permute-start | bytes 786440 | tf_op jit(solution)/shard_map/ppermute | solution.py:444
  72.2 15.9 %collective-permute-start.2 = (bf16[128,1024]{1,0:T(8,128)(2,1)S(1)}, bf16[128,1024]{1,0:T(8,128)(2,1)S(1)}, u32[]{:S(2)}, u32[]{:S(2)}) collective-permute-start(bf16[128,1024]{1,0:T(8,128)(2,1)S(1)} %collective-permute-done.odd_ref.refs_1_), channel_id=1, source_target_pairs={{0,32},{32,64},{64,96},{96,128},{128,160},{160,192},{192,224},{224... | collective-permute-start | bytes 786440 | tf_op jit(solution)/shard_map/ppermute | solution.py:451
  72.4 15.6 %collective-permute-start.3 = (bf16[128,1024]{1,0:T(8,128)(2,1)S(1)}, bf16[128,1024]{1,0:T(8,128)(2,1)S(1)}, u32[]{:S(2)}, u32[]{:S(2)}) collective-permute-start(bf16[128,1024]{1,0:T(8,128)(2,1)S(1)} %collective-permute-done.1.even_ref.refs_7_), channel_id=1, source_target_pairs={{0,224},{32,0},{64,32},{96,64},{128,96},{160,128},{192,160},{224,1... | collective-permute-start | bytes 786440 | tf_op jit(solution)/shard_map/ppermute | solution.py:452
  74.9 16.0 %collective-permute-start.4 = (bf16[128,1024]{1,0:T(8,128)(2,1)S(1)}, bf16[128,1024]{1,0:T(8,128)(2,1)S(1)}, u32[]{:S(2)}, u32[]{:S(2)}) collective-permute-start(bf16[128,1024]{1,0:T(8,128)(2,1)S(1)} %shard_map.88), channel_id=1, source_target_pairs={{0,160},{1,97},{2,162},{3,99},{4,164},{5,101},{6,166},{7,103},{8,1... | collective-permute-start | bytes 786440 | tf_op jit(solution)/shard_map/ppermute | solution.py:462
  88.0 14.7 %collective-permute-start.5 = (bf16[128,1024]{1,0:T(8,128)(2,1)S(1)}, bf16[128,1024]{1,0:T(8,128)(2,1)S(1)}, u32[]{:S(2)}, u32[]{:S(2)}) collective-permute-start(bf16[128,1024]{1,0:T(8,128)(2,1)S(1)} %collective-permute-done.2.refs_2_), channel_id=1, source_target_pairs={{0,32},{32,64},{64,96},{96,128},{128,160},{160,192},{192,224},{224... | collective-permute-start | bytes 786440 | tf_op jit(solution)/shard_map/ppermute | solution.py:451
  88.4 14.3 %collective-permute-start.6 = (bf16[128,1024]{1,0:T(8,128)(2,1)S(1)}, bf16[128,1024]{1,0:T(8,128)(2,1)S(1)}, u32[]{:S(2)}, u32[]{:S(2)}) collective-permute-start(bf16[128,1024]{1,0:T(8,128)(2,1)S(1)} %collective-permute-done.3.refs_6_), channel_id=1, source_target_pairs={{0,224},{32,0},{64,32},{96,64},{128,96},{160,128},{192,160},{224,1... | collective-permute-start | bytes 786440 | tf_op jit(solution)/shard_map/ppermute | solution.py:452
